TPU v7x, 32 devices: a whole 2x2x4 slice. The times are simulated.
32 devices in a mesh: src: 2 (over y), tile: 16 (over z, x, core).
Axes of the slice: x: 2, y: 2, z: 4, core: 2. Of those that a mesh axis runs over, the one named last changes fastest.
Arguments:
- mask_tiles: bfloat16 [16, 1024, 1024], P('tile'), may hold values from -6 to 6
- slot_pos: int32 [16], replicated, may hold values from 0 to 15, as said below
- src_shift: int32 [4, 2], P('src'), may hold values from -32 to 32
- src_weight: int32 [4], P('src'), may hold values from 1 to 8
- pupil_phase: float32 [128, 128], replicated, may hold values from -3.140625 to 3.140625
- target: bfloat16 [16, 1024, 1024], P('tile'), may hold values from 0 to 1
Outputs:
- resist: float32 [16, 1024, 1024], P('tile', 'src')
- mask_step: float32 [16, 1024, 1024], P('tile', 'src')
Inputs may be any that keep to these rules, and one draw needn't show every extreme that they name: slot_pos is a permutation of the strip positions.
All inputs are finite; a program needn't handle non-finite values.
Results may differ from a plain program's by a relative error of at most 0.0051.
Values may be sent and summed in bfloat16 or wider, within the bound.
A program may use at most 128 MiB of HBM per device.

v0:
```python
import functools
import math

import jax
import jax.numpy as jnp
import numpy as np
from jax import lax
from jax.experimental import pallas as pl
from jax.experimental.pallas import tpu as pltpu
from jax.sharding import PartitionSpec as P

TILE_PX = 1024
HALO = 64
FREQ = 128
PUPIL_R = 28
SRC_DEV = 2
EXT_PX = 1152
MESH = pl.DeviceIdType.MESH
HIGH = lax.Precision.HIGH
HIGHEST = lax.Precision.HIGHEST

steepness = 4.0
threshold = 0.6
learn_rate = 8.0


def np_tables(positions, period):
    frequency = np.arange(FREQ, dtype=np.int64) - FREQ // 2
    wrapped = np.mod(positions[:, None] * frequency[None, :], period).astype(np.float64)
    angles = wrapped * (2.0 * math.pi / period)
    return np.cos(angles).astype(np.float32), np.sin(angles).astype(np.float32)


def fdot(left, right, precision):
    return jnp.dot(left, right, precision=precision, preferred_element_type=jnp.float32)


def group_sizes(tile_count):
    low = 4 if tile_count % 4 == 0 else 1
    return low, tile_count // low


def greet(tile_count):
    low, high = group_sizes(tile_count)
    tile = lax.axis_index("tile")
    src = lax.axis_index("src")
    my_high, my_low = tile // low, tile % low
    barrier = pltpu.get_barrier_semaphore()
    for k in range(1, high):
        peer = ((my_high + k) % high) * low + my_low
        pl.semaphore_signal(barrier, inc=1, device_id={"tile": peer}, device_id_type=MESH)
    for j in range(1, low):
        peer = my_high * low + (my_low + j) % low
        pl.semaphore_signal(barrier, inc=1, device_id={"tile": peer}, device_id_type=MESH)
    src_count = lax.axis_size("src")
    for k in range(1, src_count):
        peer = (src + k) % src_count
        pl.semaphore_signal(barrier, inc=1, device_id={"src": peer}, device_id_type=MESH)
    pl.semaphore_wait(barrier, high - 1 + low - 1 + src_count - 1)


def start_high(tile_count, held, sends, recvs):
    low, high = group_sizes(tile_count)
    tile = lax.axis_index("tile")
    my_high, my_low = tile // low, tile % low
    copies = []
    for k in range(1, high):
        peer = ((my_high + k) % high) * low + my_low
        copy = pltpu.make_async_remote_copy(
            src_ref=held.at[my_low, my_high],
            dst_ref=held.at[my_low, my_high],
            send_sem=sends.at[k - 1],
            recv_sem=recvs.at[k - 1],
            device_id={"tile": peer},
            device_id_type=MESH,
        )
        copy.start()
        copies.append(copy)
    return copies


def start_low(tile_count, held, sends, recvs):
    low, high = group_sizes(tile_count)
    tile = lax.axis_index("tile")
    my_high, my_low = tile // low, tile % low
    copies = []
    for j in range(1, low):
        peer = my_high * low + (my_low + j) % low
        copy = pltpu.make_async_remote_copy(
            src_ref=held.at[my_low],
            dst_ref=held.at[my_low],
            send_sem=sends.at[j - 1],
            recv_sem=recvs.at[j - 1],
            device_id={"tile": peer},
            device_id_type=MESH,
        )
        copy.start()
        copies.append(copy)
    return copies


def pick(tile_count, held, pick_ref):
    low, high = group_sizes(tile_count)
    block = held[pick_ref[0], pick_ref[1]].astype(jnp.float32)
    return jnp.where(pick_ref[2] > 0, block, 0.0)


def start_src(held, sends, recvs):
    src = lax.axis_index("src")
    src_count = lax.axis_size("src")
    copies = []
    for k in range(1, src_count):
        copy = pltpu.make_async_remote_copy(
            src_ref=held.at[src],
            dst_ref=held.at[src],
            send_sem=sends.at[k - 1],
            recv_sem=recvs.at[k - 1],
            device_id={"src": (src + k) % src_count},
            device_id_type=MESH,
        )
        copy.start()
        copies.append(copy)
    return copies


def rim_kernel(
    tile_count, pick_ref, rim_ref, meta_ref, rims_out, meta_out,
    held, rims, meta_held, send_a, recv_a, send_b, recv_b, send_s, recv_s, send_r, recv_r
):
    low, high = group_sizes(tile_count)
    tile = lax.axis_index("tile")
    src = lax.axis_index("src")
    side = src % 2
    held[tile % low, tile // low] = rim_ref[...]
    meta_held[src] = meta_ref[...]
    greet(tile_count)
    meta_copies = start_src(meta_held, send_s, recv_s)
    for copy in start_high(tile_count, held, send_a, recv_a):
        copy.wait()
    for copy in start_low(tile_count, held, send_b, recv_b):
        copy.wait()
    rims[side] = pick(tile_count, held, pick_ref).astype(jnp.bfloat16)
    rim_copy = pltpu.make_async_remote_copy(
        src_ref=rims.at[side],
        dst_ref=rims.at[side],
        send_sem=send_r.at[0],
        recv_sem=recv_r.at[0],
        device_id={"src": src + 1 - 2 * side},
        device_id_type=MESH,
    )
    rim_copy.start()
    for copy in meta_copies:
        copy.wait()
    meta_out[...] = meta_held[...]
    rim_copy.wait()
    rims_out[...] = rims[...]


def back_kernel(
    tile_count, pick_ref, grad_ref, rim_table, own_table, out_ref,
    held, grads, total, send_a, recv_a, send_b, recv_b, send_s, recv_s
):
    low, high = group_sizes(tile_count)
    tile = lax.axis_index("tile")
    src = lax.axis_index("src")
    src_count = lax.axis_size("src")
    grads[src] = grad_ref[...]
    greet(tile_count)
    for copy in start_src(grads, send_s, recv_s):
        copy.wait()
    both = grads[0]
    for k in range(1, src_count):
        both = both + grads[k]
    total[:FREQ, :] = both
    total[FREQ:, :FREQ] = -both[:, FREQ:]
    total[FREQ:, FREQ:] = both[:, :FREQ]
    rim_back = fdot(rim_table[...], total[...], HIGHEST)
    held[tile % low, tile // low] = rim_back.astype(jnp.bfloat16)
    high_copies = start_high(tile_count, held, send_a, recv_a)
    out_ref[...] = fdot(own_table[...], total[...], HIGHEST)
    for copy in high_copies:
        copy.wait()
    for copy in start_low(tile_count, held, send_b, recv_b):
        copy.wait()
    block = pick(tile_count, held, pick_ref)
    rows = out_ref.shape[0]
    first = jnp.where(src == 0, 1.0, 0.0)
    last = jnp.where(src == src_count - 1, 1.0, 0.0)
    out_ref[:HALO, :] += first * block
    out_ref[rows - HALO :, :] += last * block


def comm_scratch(tile_count):
    low, high = group_sizes(tile_count)
    dma = pltpu.SemaphoreType.DMA
    sems = [dma((max(high - 1, 1),))] * 2 + [dma((max(low - 1, 1),))] * 2 + [dma((max(lax.axis_size("src") - 1, 1),))] * 2
    held = pltpu.VMEM((low, high, HALO, 2 * FREQ), jnp.bfloat16)
    return held, sems


def exchange_rims(tile_count, choice, rim, meta):
    held, sems = comm_scratch(tile_count)
    block = (HALO, 2 * FREQ)
    metas = (lax.axis_size("src"), *meta.shape)
    vmem = pl.BlockSpec(memory_space=pltpu.VMEM)
    return pl.pallas_call(
        functools.partial(rim_kernel, tile_count),
        out_shape=[
            jax.ShapeDtypeStruct((2, *block), jnp.bfloat16),
            jax.ShapeDtypeStruct(metas, jnp.int32),
        ],
        in_specs=[pl.BlockSpec(memory_space=pltpu.SMEM), vmem, vmem],
        out_specs=[vmem] * 2,
        scratch_shapes=[
            held,
            pltpu.VMEM((2, *block), jnp.bfloat16),
            pltpu.VMEM(metas, jnp.int32),
            *sems,
            pltpu.SemaphoreType.DMA((1,)),
            pltpu.SemaphoreType.DMA((1,)),
        ],
        compiler_params=pltpu.CompilerParams(
            collective_id=0, has_side_effects=True, vmem_limit_bytes=16 * 2**20
        ),
        cost_estimate=pl.CostEstimate(flops=0, bytes_accessed=2**20, transcendentals=0),
    )(choice, rim, meta)


def exchange_back(tile_count, choice, grad, rim_table, own_table):
    held, sems = comm_scratch(tile_count)
    vmem = pl.BlockSpec(memory_space=pltpu.VMEM)
    return pl.pallas_call(
        functools.partial(back_kernel, tile_count),
        out_shape=jax.ShapeDtypeStruct(own_table.shape, jnp.float32),
        in_specs=[pl.BlockSpec(memory_space=pltpu.SMEM), vmem, vmem, vmem],
        out_specs=vmem,
        scratch_shapes=[
            held,
            pltpu.VMEM((lax.axis_size("src"), *grad.shape), jnp.float32),
            pltpu.VMEM((2 * FREQ, 2 * FREQ), jnp.float32),
            *sems,
        ],
        compiler_params=pltpu.CompilerParams(
            collective_id=1, has_side_effects=True, vmem_limit_bytes=16 * 2**20
        ),
        cost_estimate=pl.CostEstimate(flops=10**8, bytes_accessed=2**21, transcendentals=0),
    )(choice, grad, rim_table, own_table)


def pupil_parts(shift_pair, pupil_phase, frequency):
    padded = jnp.pad(pupil_phase, FREQ)
    shift_a = shift_pair[0]
    shift_b = shift_pair[1]
    window = lax.dynamic_slice(padded, (FREQ + shift_a, FREQ + shift_b), (FREQ, FREQ))
    along_bins = frequency + shift_a
    across = frequency + shift_b
    inside = (
        along_bins[:, None] * along_bins[:, None] + across[None, :] * across[None, :]
        <= PUPIL_R * PUPIL_R
    )
    return (jnp.where(inside, jnp.cos(window), 0.0), jnp.where(inside, jnp.sin(window), 0.0))


def per_device(mask_tiles, slot_pos, src_shift, src_weight, pupil_phase, target):
    tile_count = lax.axis_size("tile")
    src_count = lax.axis_size("src")
    my_slot = lax.axis_index("tile")
    my_src = lax.axis_index("src")
    row_share = TILE_PX // src_count
    sources_total = SRC_DEV * src_count
    frequency = jnp.arange(FREQ, dtype=jnp.int32) - FREQ // 2
    col_cos, col_sin = np_tables(np.arange(TILE_PX), TILE_PX)
    row_cos, row_sin = np_tables(np.arange(EXT_PX), EXT_PX)
    col_both = np.concatenate([col_cos, col_sin], axis=1).astype(jnp.bfloat16)
    last_table = np.concatenate([col_cos.T, -col_sin.T], axis=0).astype(jnp.bfloat16)
    line_table = np.block([[col_cos.T, col_sin.T], [-col_sin.T, col_cos.T]])
    damp_table = np.ascontiguousarray(line_table.T)
    row_both = np.concatenate([row_cos, row_sin], axis=1)
    out_table = row_both[HALO : HALO + TILE_PX].astype(jnp.bfloat16)
    scale_factor = 1.0 / (FREQ / 2 * math.sqrt(EXT_PX * TILE_PX))

    slot_ids = jnp.arange(tile_count, dtype=jnp.int32)
    my_position = jnp.sum(jnp.where(slot_ids == my_slot, slot_pos, 0))
    wanted = jnp.where(my_src % 2 == 0, my_position - 1, my_position + 1)
    there = slot_pos == wanted
    wanted_slot = jnp.sum(jnp.where(there, slot_ids, 0))
    low, _ = group_sizes(tile_count)
    choice = jnp.stack(
        [wanted_slot % low, wanted_slot // low, jnp.any(there).astype(jnp.int32)]
    ).astype(jnp.int32)

    own_tile = mask_tiles[0]
    half_own = jnp.dot(own_tile, col_both, preferred_element_type=jnp.float32)
    my_rim = jnp.where(my_src % 2 == 0, half_own[TILE_PX - HALO :], half_own[:HALO])
    meta = jnp.concatenate([src_shift, src_weight[:, None]], axis=1)
    meta_block = jnp.pad(meta, ((0, 8 - SRC_DEV), (0, 128 - 3)))
    rims, metas = exchange_rims(tile_count, choice, my_rim.astype(jnp.bfloat16), meta_block)
    rims = rims.astype(jnp.float32)
    half_all = jnp.concatenate([rims[0], half_own, rims[1]], axis=0)
    meta_all = metas[:, :SRC_DEV, :3].reshape(sources_total, 3)

    spec4 = fdot(row_both.T, half_all, HIGH)
    spec_re = spec4[:FREQ, :FREQ] - spec4[FREQ:, FREQ:]
    spec_im = -spec4[:FREQ, FREQ:] - spec4[FREQ:, :FREQ]
    weights = meta_all[:, 2].astype(jnp.float32) / (4.0 * sources_total)
    pupils = [pupil_parts(meta_all[s], pupil_phase, frequency) for s in range(sources_total)]
    amps = jnp.concatenate(
        [
            jnp.concatenate(
                [
                    scale_factor * (pupil_re * spec_re - pupil_im * spec_im),
                    scale_factor * (pupil_re * spec_im + pupil_im * spec_re),
                ],
                axis=1,
            )
            for pupil_re, pupil_im in pupils
        ],
        axis=0,
    )
    lines = fdot(amps, line_table, HIGH).astype(jnp.bfloat16)

    my_table = lax.dynamic_slice_in_dim(jnp.asarray(out_table), my_src * row_share, row_share, 0)
    kept_fields = []
    intensity = jnp.zeros((row_share, TILE_PX), jnp.float32)
    for s in range(sources_total):
        top = lines[s * FREQ : (s + 1) * FREQ]
        swapped = jnp.concatenate([-top[:, TILE_PX:], top[:, :TILE_PX]], axis=1)
        stack = jnp.concatenate([top, swapped], axis=0)
        fields = jnp.dot(my_table, stack, preferred_element_type=jnp.float32)
        squared = fields * fields
        intensity = intensity + weights[s] * (squared[:, :TILE_PX] + squared[:, TILE_PX:])
        kept_fields.append(fields)
    my_target = lax.dynamic_slice_in_dim(target[0], my_src * row_share, row_share, 0).astype(
        jnp.float32
    )
    resist_rows = jax.nn.sigmoid(steepness * (intensity - threshold))
    adjoint = (
        2.0 * (resist_rows - my_target) * steepness * resist_rows * (1.0 - resist_rows)
    ).astype(jnp.bfloat16)
    adjoint_wide = jnp.concatenate([adjoint, adjoint], axis=1).astype(jnp.float32)
    dlines = []
    for s in range(sources_total):
        dfield = (2.0 * weights[s] * adjoint_wide * kept_fields[s]).astype(jnp.bfloat16)
        blocks = lax.dot_general(
            my_table, dfield, (((0,), (0,)), ((), ())), preferred_element_type=jnp.float32
        )
        dline_re = blocks[:FREQ, :TILE_PX] + blocks[FREQ:, TILE_PX:]
        dline_im = blocks[:FREQ, TILE_PX:] - blocks[FREQ:, :TILE_PX]
        dlines.append(jnp.concatenate([dline_re, dline_im], axis=1))
    damps = fdot(jnp.concatenate(dlines, axis=0), damp_table, HIGH)
    grad_re = jnp.zeros((FREQ, FREQ), jnp.float32)
    grad_im = jnp.zeros((FREQ, FREQ), jnp.float32)
    for s, (pupil_re, pupil_im) in enumerate(pupils):
        damp_re = damps[s * FREQ : (s + 1) * FREQ, :FREQ]
        damp_im = damps[s * FREQ : (s + 1) * FREQ, FREQ:]
        grad_re = grad_re + scale_factor * (pupil_re * damp_re + pupil_im * damp_im)
        grad_im = grad_im + scale_factor * (pupil_re * damp_im - pupil_im * damp_re)
    grad = jnp.concatenate([grad_re, grad_im], axis=1)

    row_array = jnp.asarray(row_both)
    own_table = lax.dynamic_slice_in_dim(row_array, HALO + my_src * row_share, row_share, 0)
    rim_start = jnp.where(my_src % 2 == 0, EXT_PX - HALO, 0)
    rim_table = lax.dynamic_slice_in_dim(row_array, rim_start, HALO, 0)
    back_rows = exchange_back(tile_count, choice, grad, rim_table, own_table)
    step_rows = jnp.dot(
        back_rows.astype(jnp.bfloat16), last_table, preferred_element_type=jnp.float32
    )
    return (resist_rows[None], (-learn_rate * step_rows)[None])


def solution(mesh):
    return jax.shard_map(
        per_device,
        mesh=mesh,
        in_specs=(P("tile", None, None), P(), P("src", None), P("src"), P(), P("tile", None, None)),
        out_specs=(P("tile", "src", None), P("tile", "src", None)),
        check_vma=False,
    )
```

profile of v0, /device:TPU:1, one launch (start us, length us, event | category | flops | bytes accessed | tf_op | source)
XLA Modules:
  0.0 117.3 jit_solution(10635336068415487474)
XLA Ops:
  0.7 1.4 %fusion.114 = s32[]{:T(128)} fusion(s32[16]{0:T(128)} %param.14, s32[]{:T(128)S(6)} %axis_index.25), kind=kLoop, calls=%fused_computation.176 | loop fusion | flops 47 | bytes 72 | tf_op jit(solution)/shard_map/reduce_sum | solution.py:283
  3.4 1.3 %fusion.113 = s32[]{:T(128)} fusion(s32[16]{0:T(128)} %param.14, s32[]{:T(128)S(6)} %select_n.100), kind=kLoop, calls=%fused_computation.175 | loop fusion | flops 47 | bytes 72 | tf_op jit(solution)/shard_map/reduce_sum | solution.py:286
  7.3 1.3 %compare_reduce_fusion = pred[]{:T(512)} fusion(s32[16]{0:T(128)} %param.14, s32[]{:T(128)S(6)} %select_n.100), kind=kLoop, calls=%fused_computation.162 | loop fusion | flops 31 | bytes 69 | tf_op jit(solution)/shard_map/reduce_or | solution.py:289
  9.3 0.1 pad_add_fusion.1.pick_ref
  9.3 1.8 %fusion.49 = f32[256,1024]{1,0:T(8,128)S(1)} fusion(bf16[1024,256]{1,0:T(8,128)(2,1)} %constant.117.clone, bf16[1,1024,1024]{2,1,0:T(8,128)(2,1)S(1)} %copy-done), kind=kOutput, calls=%fused_computation.56 | convolution fusion | flops 536870912 | bytes 3670016 | tf_op jit(solution)/shard_map/dot_general | solution.py:293
  11.2 0.2 copy.15
  11.5 0.1 copy.16
  11.5 0.1 pad_add_fusion
  11.6 18.0 %shard_map.140 = (bf16[2,64,256]{2,1,0:T(8,128)(2,1)S(1)}, s32[2,8,128]{2,1,0:T(8,128)S(1)}) custom-call(s32[3]{0:T(128)S(1)} %pad_add_fusion.1.pick_ref, bf16[64,256]{1,0:T(8,128)(2,1)S(1)} %fusion.104.rim_ref, s32[8,128]{1,0:T(8,128)S(1)} %pad.11.meta_ref), custom_call_target="tpu_custom_call" | custom-call | bytes 1048576 | tf_op jit(solution)/shard_map/pallas_call | solution.py:206
  29.6 0.7 fusion.128
  30.3 1.2 %add_multiply_fusion.8 = (s32[128]{0:T(128)S(1)}, s32[128]{0:T(128)S(1)}) fusion(s32[]{:T(128)} %bitcast.16, s32[]{:T(128)} %bitcast.15), kind=kLoop, calls=%fused_computation.180 | loop fusion | flops 640 | bytes 1032 | tf_op jit(solution)/shard_map/mul | solution.py:258
  34.0 0.7 fusion.133
  34.7 0.2 convolution_add_fusion.1
  35.0 0.2 fusion.55
  35.2 1.2 %add_multiply_fusion.12 = (s32[128]{0:T(128)S(1)}, s32[128]{0:T(128)S(1)}) fusion(s32[]{:T(128)} %bitcast.9, s32[]{:T(128)} %bitcast.8), kind=kLoop, calls=%fused_computation.184 | loop fusion | flops 640 | bytes 1032 | tf_op jit(solution)/shard_map/mul | solution.py:258
  38.8 0.3 subtract_multiply_fusion.3
  39.1 0.6 subtract_multiply_fusion.1
  39.7 1.3 %add_multiply_fusion.6 = (s32[128]{0:T(128)S(1)}, s32[128]{0:T(128)S(1)}) fusion(s32[]{:T(128)} %bitcast.18, s32[]{:T(128)} %bitcast.17), kind=kLoop, calls=%fused_computation.178 | loop fusion | flops 640 | bytes 1032 | tf_op jit(solution)/shard_map/mul | solution.py:258
  43.5 1.3 %add_multiply_fusion.10 = (s32[128]{0:T(128)S(1)}, s32[128]{0:T(128)S(1)}) fusion(s32[]{:T(128)} %bitcast.14, s32[]{:T(128)} %bitcast.13), kind=kLoop, calls=%fused_computation.182 | loop fusion | flops 640 | bytes 1032 | tf_op jit(solution)/shard_map/mul | solution.py:258
  47.5 1.5 %subtract_multiply_fusion.2 = (f32[128,128]{1,0:T(8,128)S(1)}, f32[128,128]{1,0:T(8,128)S(1)}, f32[128,128]{1,0:T(8,128)S(1)}, f32[128,128]{1,0:T(8,128)S(1)}, f32[128,128]{1,0:T(8,128)S(1)}) fusion(f32[128,128]{1,0:T(8,128)S(1)} %get-tuple-element.9, f32[128,128]{1,0:T(8,128)S(1)} %get-tuple-element.10, s32[]{:T(128)S(6)} %select_n.111, s32[]{:T(128)S(6)} %select_n.112, ...), kind=kLoop, calls=%fused_computation.151 | loop fusion | flops 589824 | bytes 527384 | tf_op jit(solution)/shard_map/mul | solution.py:311
  49.0 3.5 %convolution_convert_fusion = bf16[512,2048]{1,0:T(8,128)(2,1)S(1)} fusion(f32[256,2048]{1,0:T(8,128)} %constant.119.clone, f32[128,128]{1,0:T(8,128)S(1)} %get-tuple-element.39, f32[128,128]{1,0:T(8,128)S(1)} %get-tuple-element.40, f32[128,128]{1,0:T(8,128)S(1)} %get-tuple-element.34, f32[128,128]{1,0:T(8,128)S(1)} %get-tuple-element.33, ...), kind=kOutput, calls=%fused_computation.28 | convolution fusion | flops 1612578816 | bytes 4718592 | tf_op jit(solution)/shard_map/dot_general | solution.py:35
  52.5 1.2 %fusion.126 = (bf16[128,2048]{1,0:T(8,128)(2,1)}, bf16[128,2048]{1,0:T(8,128)(2,1)S(1)}, bf16[128,2048]{1,0:T(8,128)(2,1)}, bf16[128,2048]{1,0:T(8,128)(2,1)}) fusion(bf16[512,2048]{1,0:T(8,128)(2,1)S(1)} %convolution_convert_fusion), kind=kLoop, calls=%fused_computation.197 | loop fusion | bytes 4194304 | tf_op jit(solution)/shard_map/slice | solution.py:326
  53.7 1.3 %slice_negate_fusion.3 = (bf16[128,1024]{1,0:T(8,128)(2,1)}, bf16[128,1024]{1,0:T(8,128)(2,1)S(1)}, bf16[128,1024]{1,0:T(8,128)(2,1)}, bf16[128,1024]{1,0:T(8,12...) fusion(bf16[512,2048]{1,0:T(8,128)(2,1)S(1)} %convolution_conve, ...), kind=kLoop, calls=%fused_computation.128 | loop fusion | flops 524288 | bytes 4194304 | tf_op jit(solution)/shard_map/neg | solution.py:327
  55.0 4.0 %fusion.131 = (f32[512,2048]{1,0:T(8,128)S(1)}, f32[512,2048]{1,0:T(8,128)}) fusion(bf16[128,1024]{1,0:T(8,128)(2,1)} %get-tuple-element.28, bf16[128,1024]{1,0:T(8,128)(2,1)} %get-tuple-element.29, bf16[128,2048]{1,0:T(8,128)(2,1)} %get-tuple-element.22, bf16[1024,256]{1,0:T(8,128)(2,1)S(1)} %copy-done.2, s32[]{:T(128)S(6)} %select_n.106), kind=kOutput, calls=%fused_computation.202 | convolution fusion | flops 541065216 | bytes 9699332 | tf_op jit(solution)/shard_map/dot_general | solution.py:329
  59.1 2.7 %fusion.132 = (f32[512,2048]{1,0:T(8,128)S(1)}, f32[512,2048]{1,0:T(8,128)}) fusion(bf16[128,1024]{1,0:T(8,128)(2,1)S(1)} %copy-done.10, bf16[128,1024]{1,0:T(8,128)(2,1)S(1)} %copy-done.9, bf16[128,2048]{1,0:T(8,128)(2,1)S(1)} %copy-done.4, bf16[1024,256]{1,0:T(8,128)(2,1)S(1)} %copy-done.2, s32[]{:T(128)S(6)} %select_n.106), kind=kOutput, calls=%fused_computation.203 | convolution fusion | flops 541065216 | bytes 9699332 | tf_op jit(solution)/shard_map/dot_general | solution.py:329
  61.7 2.7 %fusion.130 = (f32[512,2048]{1,0:T(8,128)S(1)}, f32[512,2048]{1,0:T(8,128)}) fusion(bf16[128,1024]{1,0:T(8,128)(2,1)S(1)} %copy-done.7, bf16[128,1024]{1,0:T(8,128)(2,1)S(1)} %copy-done.8, bf16[128,2048]{1,0:T(8,128)(2,1)S(1)} %copy-done.3, bf16[1024,256]{1,0:T(8,128)(2,1)S(1)} %copy-done.2, s32[]{:T(128)S(6)} %select_n.106), kind=kOutput, calls=%fused_computation.201 | convolution fusion | flops 541065216 | bytes 9699332 | tf_op jit(solution)/shard_map/dot_general | solution.py:329
  64.5 2.7 %fusion.129 = (f32[512,2048]{1,0:T(8,128)S(1)}, f32[512,2048]{1,0:T(8,128)}) fusion(bf16[128,1024]{1,0:T(8,128)(2,1)S(1)} %get-tuple-element.24, bf16[128,1024]{1,0:T(8,128)(2,1)S(1)} %copy-done.6, bf16[128,2048]{1,0:T(8,128)(2,1)S(1)} %get-tuple-element.20, bf16[1024,256]{1,0:T(8,128)(2,1)S(1)} %copy-done.2, s32[]{:T(128)S(6)} %select_n.106), kind=kOutput, calls=%fused_computation.200 | convolution fusion | flops 541065216 | bytes 9699332 | tf_op jit(solution)/shard_map/dot_general | solution.py:329
  67.2 0.1 convert_multiply_fusion.4
  67.3 0.6 fusion.127
  67.9 5.8 %fusion.48 = (bf16[512,1024]{1,0:T(8,128)(2,1)S(1)}, f32[512,1024]{1,0:T(8,128)}) fusion(bf16[1,1024,1024]{2,1,0:T(8,128)(2,1)S(1)} %copy-done.12, s32[]{:T(128)S(6)} %select_n.106, f32[512,2048]{1,0:T(8,128)S(1)} %get-tuple-element.53, f32[]{:T(128)} %bitcast.21, f32[512,2048]{1,0:T(8,128)S(1)} %get-tuple-element.55, f32[]{:T(128)} %bitcast.20, ...), kind=kLoop, calls=%fused_computation.55 | loop fusion | flops 12058624 | bytes 20971540 | tf_op jit(solution)/shard_map/convert_element_type | solution.py:339
  74.3 3.0 %fusion.30 = f32[256,2048]{1,0:T(8,128)S(1)} fusion(f32[512,2048]{1,0:T(8,128)} %get-tuple-element.60, f32[]{:T(128)S(6)} %mul.365, bf16[512,1024]{1,0:T(8,128)(2,1)S(1)} %get-tuple-element.6, bf16[1024,256]{1,0:T(8,128)(2,1)S(1)} %copy-done.2, s32[]{:T(128)S(6)} %select_n.106), kind=kOutput, calls=%fused_computation.32 | convolution fusion | flops 544210944 | bytes 7602184 | tf_op jit(solution)/shard_map/dot_general | solution.py:344
  77.2 0.1 slice_add_fusion.7
  78.0 3.0 %fusion.28 = f32[256,2048]{1,0:T(8,128)S(1)} fusion(f32[512,2048]{1,0:T(8,128)} %get-tuple-element.58, f32[]{:T(128)S(6)} %mul.373, bf16[512,1024]{1,0:T(8,128)(2,1)S(1)} %get-tuple-element.6, bf16[1024,256]{1,0:T(8,128)(2,1)S(1)} %copy-done.2, s32[]{:T(128)S(6)} %select_n.106), kind=kOutput, calls=%fused_computation.31 | convolution fusion | flops 544210944 | bytes 7602184 | tf_op jit(solution)/shard_map/dot_general | solution.py:344
  80.9 0.9 slice_add_fusion.6
  82.5 3.0 %fusion.26 = f32[256,2048]{1,0:T(8,128)S(1)} fusion(f32[512,2048]{1,0:T(8,128)} %get-tuple-element.56, f32[]{:T(128)S(6)} %mul.377, bf16[512,1024]{1,0:T(8,128)(2,1)S(1)} %get-tuple-element.6, bf16[1024,256]{1,0:T(8,128)(2,1)S(1)} %copy-done.2, s32[]{:T(128)S(6)} %select_n.106), kind=kOutput, calls=%fused_computation.30 | convolution fusion | flops 544210944 | bytes 7602184 | tf_op jit(solution)/shard_map/dot_general | solution.py:344
  85.5 1.1 slice_add_fusion.5
  87.3 3.1 %fusion.24 = f32[256,2048]{1,0:T(8,128)S(1)} fusion(f32[512,2048]{1,0:T(8,128)} %get-tuple-element.54, f32[]{:T(128)S(6)} %mul.381, bf16[512,1024]{1,0:T(8,128)(2,1)S(1)} %get-tuple-element.6, bf16[1024,256]{1,0:T(8,128)(2,1)S(1)} %copy-done.2, s32[]{:T(128)S(6)} %select_n.106), kind=kOutput, calls=%fused_computation.29 | convolution fusion | flops 544210944 | bytes 7602184 | tf_op jit(solution)/shard_map/dot_general | solution.py:344
  90.4 0.1 slice_add_fusion.4
  90.6 0.9 copy-done.14
  91.4 0.2 copy-done.15
  91.6 0.2 copy-done.16
  91.7 1.9 %fusion.8 = f32[512,256]{1,0:T(8,128)S(1)} fusion(f32[2048,256]{1,0:T(8,128)S(1)} %copy-done.21, f32[128,1024]{1,0:T(8,128)S(1)} %get-tuple-element.18, f32[128,1024]{1,0:T(8,128)S(1)} %get-tuple-element.17, f32[128,1024]{1,0:T(8,128)S(1)} %copy-done.16, f32[128,1024]{1,0:T(8,128)S(1)} %copy-done.15, f32[128,1024]{1,0:T(8,128)S(1)} %copy-done.14, ...), kind=kOutput, calls=%fused_computation.12 | convolution fusion | flops 1617952768 | bytes 6815744 | tf_op jit(solution)/shard_map/dot_general | solution.py:35
  93.7 1.3 %add_multiply_fusion.1 = f32[128,128]{1,0:T(8,128)S(1)} fusion(f32[512,256]{1,0:T(8,128)S(1)} %fusion.8, s32[]{:T(128)S(6)} %select_n.107, s32[]{:T(128)S(6)} %select_n.108, f32[128,128]{1,0:T(8,128)S(1)} %copy-done.5, s32[128]{0:T(128)S(1)} %get-tuple-element.61, s32[128]{0:T(128)S(1)} %get-tuple-element.62, s32[]{:T(128)S(6)} %select_n.111, ...), kind=kLoop, calls=%fused_computation.139 | loop fusion | flops 524288 | bytes 659488 | tf_op jit(solution)/shard_map/add | solution.py:356
  95.0 1.3 %add_multiply_fusion = f32[128,128]{1,0:T(8,128)S(1)} fusion(f32[512,256]{1,0:T(8,128)S(1)} %fusion.8, s32[]{:T(128)S(6)} %select_n.107, s32[]{:T(128)S(6)} %select_n.108, f32[128,128]{1,0:T(8,128)S(1)} %copy-done.5, s32[128]{0:T(128)S(1)} %get-tuple-element.61, s32[128]{0:T(128)S(1)} %get-tuple-element.62, s32[]{:T(128)S(6)} %select_n.111, ...), kind=kLoop, calls=%fused_computation.138 | loop fusion | flops 524288 | bytes 659488 | tf_op jit(solution)/shard_map/add | solution.py:357
  96.4 0.9 constant_dynamic-slice_fusion.1.rim_table
  97.2 1.2 %constant_dynamic-slice_fusion.own_table = f32[512,256]{1,0:T(8,128)S(1)} fusion(f32[1152,256]{1,0:T(8,128)} %constant.122.clone, s32[]{:T(128)S(6)} %select_n.124), kind=kLoop, calls=%fused_computation.172 | loop fusion | bytes 1048580 | tf_op jit(solution)/shard_map/dynamic_slice | solution.py:361
  98.4 17.1 %shard_map.141 = f32[512,256]{1,0:T(8,128)S(1)} custom-call(s32[3]{0:T(128)S(1)} %pad_add_fusion.1.pick_ref, f32[128,256]{1,0:T(8,128)S(1)} %pad_maximum_fusion.5.grad_ref, f32[64,256]{1,0:T(8,128)S(1)} %constant_dynamic-slice_fusion.1.rim_table, f32[512,256]{1,0:T(8,128)S(1)} %constant_dynamic-slice_fusion.own_table), custom_call_target="tpu_custom_call" | custom-call | flops 100000000 | bytes 2097152 | tf_op jit(solution)/shard_map/pallas_call | solution.py:232
  115.5 1.8 %multiply_bitcast_fusion = f32[1,512,1024]{2,1,0:T(8,128)} fusion(bf16[256,1024]{1,0:T(8,128)(2,1)S(1)} %copy-done.13, f32[512,256]{1,0:T(8,128)S(1)} %shard_map.141), kind=kOutput, calls=%fused_computation.58 | convolution fusion | flops 269090816 | bytes 3145728 | tf_op jit(solution)/shard_map/dot_general | solution.py:365
  (46 shorter events, 0.2 us)
Async XLA Ops:
  0.6 8.7 %copy-start = (bf16[1,1024,1024]{2,1,0:T(8,128)(2,1)S(1)}, bf16[1,1024,1024]{2,1,0:T(8,128)(2,1)}, u32[]{:S(2)}) copy-start(bf16[1,1024,1024]{2,1,0:T(8,128)(2,1)} %param.13) | copy-start | bytes 6291460
  9.3 2.1 %copy-start.20 = (s32[2]{0:T(128)S(1)}, s32[2]{0:T(128)}, u32[]{:S(2)}) copy-start(s32[2]{0:T(128)} %param.16) | copy-start | bytes 28
  9.3 2.2 %copy-start.19 = (s32[2,2]{1,0:T(2,128)S(1)}, s32[2,2]{1,0:T(2,128)}, u32[]{:S(2)}) copy-start(s32[2,2]{1,0:T(2,128)} %param.15) | copy-start | bytes 52
  11.2 22.8 %copy-start.11 = (f32[256,1024]{1,0:T(8,128)S(1)}, f32[256,1024]{1,0:T(8,128)}, u32[]{:S(2)}) copy-start(f32[256,1024]{1,0:T(8,128)} %constant.131) | copy-start | bytes 3145732
  11.2 23.5 %copy-start.18 = (f32[256,64]{1,0:T(8,128)S(1)}, f32[256,64]{1,0:T(8,128)}, u32[]{:S(2)}) copy-start(f32[256,64]{1,0:T(8,128)} %constant.130) | copy-start | bytes 196612
  11.4 23.5 %copy-start.17 = (f32[256,64]{1,0:T(8,128)S(1)}, f32[256,64]{1,0:T(8,128)}, u32[]{:S(2)}) copy-start(f32[256,64]{1,0:T(8,128)} %constant.132) | copy-start | bytes 196612
  11.4 27.4 %copy-start.5 = (f32[128,128]{1,0:T(8,128)S(1)}, f32[128,128]{1,0:T(8,128)}, u32[]{:S(2)}) copy-start(f32[128,128]{1,0:T(8,128)} %param.17) | copy-start | bytes 196612
  53.7 1.3 %copy-start.2 = (bf16[1024,256]{1,0:T(8,128)(2,1)S(1)}, bf16[1024,256]{1,0:T(8,128)(2,1)}, u32[]{:S(2)}) copy-start(bf16[1024,256]{1,0:T(8,128)(2,1)} %constant.120.clone) | copy-start | bytes 1572868
  55.0 4.0 %copy-start.4 = (bf16[128,2048]{1,0:T(8,128)(2,1)S(1)}, bf16[128,2048]{1,0:T(8,128)(2,1)}, u32[]{:S(2)}) copy-start(bf16[128,2048]{1,0:T(8,128)(2,1)} %get-tuple-element.19) | copy-start | bytes 1572868
  55.0 4.0 %copy-start.9 = (bf16[128,1024]{1,0:T(8,128)(2,1)S(1)}, bf16[128,1024]{1,0:T(8,128)(2,1)}, u32[]{:S(2)}) copy-start(bf16[128,1024]{1,0:T(8,128)(2,1)} %get-tuple-element.23) | copy-start | bytes 786436
  55.0 4.0 %copy-start.10 = (bf16[128,1024]{1,0:T(8,128)(2,1)S(1)}, bf16[128,1024]{1,0:T(8,128)(2,1)}, u32[]{:S(2)}) copy-start(bf16[128,1024]{1,0:T(8,128)(2,1)} %get-tuple-element.30) | copy-start | bytes 786436
  59.0 2.7 %copy-start.3 = (bf16[128,2048]{1,0:T(8,128)(2,1)S(1)}, bf16[128,2048]{1,0:T(8,128)(2,1)}, u32[]{:S(2)}) copy-start(bf16[128,2048]{1,0:T(8,128)(2,1)} %get-tuple-element.21) | copy-start | bytes 1572868
  59.0 2.7 %copy-start.7 = (bf16[128,1024]{1,0:T(8,128)(2,1)S(1)}, bf16[128,1024]{1,0:T(8,128)(2,1)}, u32[]{:S(2)}) copy-start(bf16[128,1024]{1,0:T(8,128)(2,1)} %get-tuple-element.26) | copy-start | bytes 786436
  59.0 2.7 %copy-start.8 = (bf16[128,1024]{1,0:T(8,128)(2,1)S(1)}, bf16[128,1024]{1,0:T(8,128)(2,1)}, u32[]{:S(2)}) copy-start(bf16[128,1024]{1,0:T(8,128)(2,1)} %get-tuple-element.27) | copy-start | bytes 786436
  61.7 2.7 %copy-start.6 = (bf16[128,1024]{1,0:T(8,128)(2,1)S(1)}, bf16[128,1024]{1,0:T(8,128)(2,1)}, u32[]{:S(2)}) copy-start(bf16[128,1024]{1,0:T(8,128)(2,1)} %get-tuple-element.25) | copy-start | bytes 786436
  64.4 3.4 %copy-start.12 = (bf16[1,1024,1024]{2,1,0:T(8,128)(2,1)S(1)}, bf16[1,1024,1024]{2,1,0:T(8,128)(2,1)}, u32[]{:S(2)}) copy-start(bf16[1,1024,1024]{2,1,0:T(8,128)(2,1)} %param.18) | copy-start | bytes 6291460
  87.2 3.3 %copy-start.21 = (f32[2048,256]{1,0:T(8,128)S(1)}, f32[2048,256]{1,0:T(8,128)}, u32[]{:S(2)}) copy-start(f32[2048,256]{1,0:T(8,128)} %constant.121.clone) | copy-start | bytes 6291460
  90.4 1.0 copy-start.14
  90.4 1.2 %copy-start.15 = (f32[128,1024]{1,0:T(8,128)S(1)}, f32[128,1024]{1,0:T(8,128)}, u32[]{:S(2)}) copy-start(f32[128,1024]{1,0:T(8,128)} %get-tuple-element.15) | copy-start | bytes 1572868
  90.4 1.3 %copy-start.16 = (f32[128,1024]{1,0:T(8,128)S(1)}, f32[128,1024]{1,0:T(8,128)}, u32[]{:S(2)}) copy-start(f32[128,1024]{1,0:T(8,128)} %get-tuple-element.16) | copy-start | bytes 1572868
  93.7 21.8 %copy-start.13 = (bf16[256,1024]{1,0:T(8,128)(2,1)S(1)}, bf16[256,1024]{1,0:T(8,128)(2,1)}, u32[]{:S(2)}) copy-start(bf16[256,1024]{1,0:T(8,128)(2,1)} %constant.123.clone) | copy-start | bytes 1572868
  97.2 20.1 %copy-start.1 = (bf16[1,1024,1024]{2,1,0:T(8,128)(2,1)S(1)}, bf16[1,1024,1024]{2,1,0:T(8,128)(2,1)}, u32[]{:S(2)}) copy-start(bf16[1,1024,1024]{2,1,0:T(8,128)(2,1)} %param.13) | copy-start | bytes 6291460
where the time goes:
time: 118 us; the launch traced here: 117 us
  Pallas kernels  35 us (30%)
  matrix products  34.2 us (29%)
  other arithmetic  23.7 us (20%)
  between operations  18.2 us (15%)
  local copies, waits for them, and re-layouts  6.18 us (5%)
    pallas_call x1, Pallas kernels, exchange_rims(): pl.pallas_call(functools.partial(rim_kernel, tile_count), out_shape=[jax....  18 us
    pallas_call x1, Pallas kernels, exchange_back(): pl.pallas_call(functools.partial(back_kernel, tile_count), out_shape=jax....  17.1 us
    dot_general x4, matrix products, per_device(): fields = jnp.dot(my_table, stack, preferred_element_type=jnp.float32)  12.1 us
    dot_general x4, matrix products, per_device(): lax.dot_general(my_table, dfield, (((0,), (0,)), ((), ())), preferred_ele...  12 us
    dot_general x5, matrix products, fdot(): jnp.dot(left, right, precision=precision, preferred_element_type=jnp.floa...  6.53 us
    convert_element_type x1, other arithmetic, per_device(): adjoint = (2.0 * (resist_rows - my_target) * steepness * resist_rows * (1...  5.75 us
    mul x4, other arithmetic, pupil_parts(): across[None, :] * across[None, :]  5.01 us
    mul x3, other arithmetic, per_device(): scale_factor * (pupil_re * spec_re - pupil_im * spec_im)  2.41 us

commit v1 on v0

v1 whole, which is shorter than its diff:
```python
import functools
import math

import jax
import jax.numpy as jnp
import numpy as np
from jax import lax
from jax.experimental import pallas as pl
from jax.experimental.pallas import tpu as pltpu
from jax.sharding import PartitionSpec as P

TILE_PX = 1024
HALO = 64
FREQ = 128
PUPIL_R = 28
SRC_DEV = 2
EXT_PX = 1152
MESH = pl.DeviceIdType.MESH
HIGHEST = lax.Precision.HIGHEST

steepness = 4.0
threshold = 0.6
learn_rate = 8.0


def np_tables(positions, period):
    frequency = np.arange(FREQ, dtype=np.int64) - FREQ // 2
    wrapped = np.mod(positions[:, None] * frequency[None, :], period).astype(np.float64)
    angles = wrapped * (2.0 * math.pi / period)
    return np.cos(angles).astype(np.float32), np.sin(angles).astype(np.float32)


def fdot(left, right, precision):
    return jnp.dot(left, right, precision=precision, preferred_element_type=jnp.float32)


def group_sizes(tile_count):
    low = 4 if tile_count % 4 == 0 else 1
    return low, tile_count // low


def greet(tile_count):
    low, high = group_sizes(tile_count)
    tile = lax.axis_index("tile")
    src = lax.axis_index("src")
    my_high, my_low = tile // low, tile % low
    barrier = pltpu.get_barrier_semaphore()
    src_count = lax.axis_size("src")
    for k in range(1, high):
        peer = ((my_high + k) % high) * low + my_low
        pl.semaphore_signal(barrier, inc=1, device_id={"tile": peer}, device_id_type=MESH)
    for j in range(1, low):
        peer = my_high * low + (my_low + j) % low
        pl.semaphore_signal(barrier, inc=1, device_id={"tile": peer}, device_id_type=MESH)
    for k in range(1, src_count):
        peer = (src + k) % src_count
        pl.semaphore_signal(barrier, inc=1, device_id={"src": peer}, device_id_type=MESH)
    pl.semaphore_wait(barrier, high - 1 + low - 1 + src_count - 1)


def start_high(tile_count, held, sends, recvs):
    low, high = group_sizes(tile_count)
    tile = lax.axis_index("tile")
    my_high, my_low = tile // low, tile % low
    copies = []
    for k in range(1, high):
        peer = ((my_high + k) % high) * low + my_low
        copy = pltpu.make_async_remote_copy(
            src_ref=held.at[my_low, my_high],
            dst_ref=held.at[my_low, my_high],
            send_sem=sends.at[k - 1],
            recv_sem=recvs.at[k - 1],
            device_id={"tile": peer},
            device_id_type=MESH,
        )
        copy.start()
        copies.append(copy)
    return copies


def start_low(tile_count, held, sends, recvs):
    low, high = group_sizes(tile_count)
    tile = lax.axis_index("tile")
    my_high, my_low = tile // low, tile % low
    copies = []
    for j in range(1, low):
        peer = my_high * low + (my_low + j) % low
        copy = pltpu.make_async_remote_copy(
            src_ref=held.at[my_low],
            dst_ref=held.at[my_low],
            send_sem=sends.at[j - 1],
            recv_sem=recvs.at[j - 1],
            device_id={"tile": peer},
            device_id_type=MESH,
        )
        copy.start()
        copies.append(copy)
    return copies


def pick(tile_count, held, pos_ref):
    low, _ = group_sizes(tile_count)
    side = lax.axis_index("src") % 2
    wanted = pos_ref[lax.axis_index("tile")] - 1 + 2 * side
    slot = jnp.int32(0)
    found = jnp.int32(0)
    for i in range(tile_count):
        hit = pos_ref[i] == wanted
        slot = slot + jnp.where(hit, i, 0)
        found = found + jnp.where(hit, 1, 0)
    block = held[slot % low, slot // low].astype(jnp.float32)
    return jnp.where(found > 0, block, 0.0)


def start_src(held, sends, recvs):
    src = lax.axis_index("src")
    src_count = lax.axis_size("src")
    copies = []
    for k in range(1, src_count):
        copy = pltpu.make_async_remote_copy(
            src_ref=held.at[src],
            dst_ref=held.at[src],
            send_sem=sends.at[k - 1],
            recv_sem=recvs.at[k - 1],
            device_id={"src": (src + k) % src_count},
            device_id_type=MESH,
        )
        copy.start()
        copies.append(copy)
    return copies


def rim_kernel(
    tile_count, pos_ref, shift_ref, weight_ref, mask_ref, table_ref, rims_out, meta_out, half_out,
    held, rims, meta_held, send_a, recv_a, send_b, recv_b, send_s, recv_s, send_r, recv_r
):
    low, high = group_sizes(tile_count)
    tile = lax.axis_index("tile")
    src = lax.axis_index("src")
    side = src % 2
    row = lax.broadcasted_iota(jnp.int32, (8, 128), 0)
    col = lax.broadcasted_iota(jnp.int32, (8, 128), 1)
    meta = jnp.zeros((8, 128), jnp.int32)
    for p in range(SRC_DEV):
        meta = jnp.where((row == p) & (col == 0), shift_ref[p, 0], meta)
        meta = jnp.where((row == p) & (col == 1), shift_ref[p, 1], meta)
        meta = jnp.where((row == p) & (col == 2), weight_ref[p], meta)
    meta_held[src] = meta
    start = pl.multiple_of((1 - side) * (TILE_PX - HALO), HALO)
    rim = jnp.dot(
        mask_ref[0, pl.ds(start, HALO), :], table_ref[...], preferred_element_type=jnp.float32
    )
    held[tile % low, tile // low] = rim.astype(jnp.bfloat16)
    greet(tile_count)
    high_copies = start_high(tile_count, held, send_a, recv_a)
    meta_copies = start_src(meta_held, send_s, recv_s)
    for copy in high_copies:
        copy.wait()
    low_copies = start_low(tile_count, held, send_b, recv_b)

    def transform(i, carry):
        at = pl.ds(pl.multiple_of(i * 256, 256), 256)
        half_out[at, :] = jnp.dot(
            mask_ref[0, at, :], table_ref[...], preferred_element_type=jnp.float32
        )
        return carry

    lax.fori_loop(0, TILE_PX // 256, transform, 0)
    for copy in low_copies:
        copy.wait()
    rims[side] = pick(tile_count, held, pos_ref).astype(jnp.bfloat16)
    rim_copy = pltpu.make_async_remote_copy(
        src_ref=rims.at[side],
        dst_ref=rims.at[side],
        send_sem=send_r.at[0],
        recv_sem=recv_r.at[0],
        device_id={"src": src + 1 - 2 * side},
        device_id_type=MESH,
    )
    rim_copy.start()
    for copy in meta_copies:
        copy.wait()
    meta_out[...] = meta_held[...]
    rim_copy.wait()
    rims_out[...] = rims[...]


def back_kernel(
    tile_count, pos_ref, grad_ref, rim_table, own_table, out_ref,
    held, grads, total, send_a, recv_a, send_b, recv_b, send_s, recv_s
):
    low, high = group_sizes(tile_count)
    tile = lax.axis_index("tile")
    src = lax.axis_index("src")
    src_count = lax.axis_size("src")
    grads[src] = grad_ref[...]
    greet(tile_count)
    for copy in start_src(grads, send_s, recv_s):
        copy.wait()
    both = grads[0]
    for k in range(1, src_count):
        both = both + grads[k]
    total[:FREQ, :] = both
    total[FREQ:, :FREQ] = -both[:, FREQ:]
    total[FREQ:, FREQ:] = both[:, :FREQ]
    rim_back = fdot(rim_table[...], total[...], HIGHEST)
    held[tile % low, tile // low] = rim_back.astype(jnp.bfloat16)
    high_copies = start_high(tile_count, held, send_a, recv_a)
    out_ref[...] = fdot(own_table[...], total[...], HIGHEST)
    for copy in high_copies:
        copy.wait()
    for copy in start_low(tile_count, held, send_b, recv_b):
        copy.wait()
    block = pick(tile_count, held, pos_ref)
    rows = out_ref.shape[0]
    first = jnp.where(src == 0, 1.0, 0.0)
    last = jnp.where(src == src_count - 1, 1.0, 0.0)
    out_ref[:HALO, :] += first * block
    out_ref[rows - HALO :, :] += last * block


def comm_scratch(tile_count):
    low, high = group_sizes(tile_count)
    dma = pltpu.SemaphoreType.DMA
    sems = [dma((max(high - 1, 1),))] * 2 + [dma((max(low - 1, 1),))] * 2 + [dma((max(lax.axis_size("src") - 1, 1),))] * 2
    held = pltpu.VMEM((low, high, HALO, 2 * FREQ), jnp.bfloat16)
    return held, sems


def exchange_rims(tile_count, slot_pos, src_shift, src_weight, mask_tiles, table):
    held, sems = comm_scratch(tile_count)
    block = (HALO, 2 * FREQ)
    metas = (lax.axis_size("src"), 8, 128)
    vmem = pl.BlockSpec(memory_space=pltpu.VMEM)
    smem = pl.BlockSpec(memory_space=pltpu.SMEM)
    return pl.pallas_call(
        functools.partial(rim_kernel, tile_count),
        out_shape=[
            jax.ShapeDtypeStruct((2, *block), jnp.bfloat16),
            jax.ShapeDtypeStruct(metas, jnp.int32),
            jax.ShapeDtypeStruct((TILE_PX, 2 * FREQ), jnp.float32),
        ],
        in_specs=[smem, smem, smem, vmem, vmem],
        out_specs=[vmem] * 3,
        scratch_shapes=[
            held,
            pltpu.VMEM((2, *block), jnp.bfloat16),
            pltpu.VMEM(metas, jnp.int32),
            *sems,
            pltpu.SemaphoreType.DMA((1,)),
            pltpu.SemaphoreType.DMA((1,)),
        ],
        compiler_params=pltpu.CompilerParams(
            collective_id=0, has_side_effects=True, vmem_limit_bytes=24 * 2**20
        ),
        cost_estimate=pl.CostEstimate(flops=6 * 10**8, bytes_accessed=2**22, transcendentals=0),
    )(slot_pos, src_shift, src_weight, mask_tiles, table)


def split(value):
    top = value.astype(jnp.bfloat16)
    return top, (value - top.astype(jnp.float32)).astype(jnp.bfloat16)


def np_split(value):
    top = value.astype(jnp.bfloat16)
    return top, (value - top.astype(np.float32)).astype(jnp.bfloat16)


def bdot(left, right):
    return jnp.dot(left, right, preferred_element_type=jnp.float32)


def bdot_t(left, right):
    return lax.dot_general(
        left, right, (((1,), (1,)), ((), ())), preferred_element_type=jnp.float32
    )


def image_kernel(
    sources_total, scale_factor, place_ref, meta_ref,
    half_ref, rims_ref, own_top, own_low, rim_top, rim_low, phase_ref, line_top, line_low,
    table_ref, table_t_ref, target_ref, resist_ref, grad_ref,
    pupil_re, pupil_im, amp_top, amp_low, fields, damps, dlines
):
    step = pl.program_id(0)
    width = target_ref.shape[2]

    @pl.when(step == 0)
    def _():
        half_top, half_low = split(half_ref[...])
        spec4 = bdot(own_top[...], half_top)
        spec4 += bdot(own_top[...], half_low) + bdot(own_low[...], half_top)
        rims = rims_ref[...].reshape(2 * HALO, 2 * FREQ)
        spec4 += bdot(rim_top[...], rims) + bdot(rim_low[...], rims)
        spec_re = scale_factor * (spec4[:FREQ, :FREQ] - spec4[FREQ:, FREQ:])
        spec_im = -scale_factor * (spec4[:FREQ, FREQ:] + spec4[FREQ:, :FREQ])
        f_a = lax.broadcasted_iota(jnp.int32, (FREQ, FREQ), 0) - FREQ // 2
        f_b = lax.broadcasted_iota(jnp.int32, (FREQ, FREQ), 1) - FREQ // 2
        inside = f_a * f_a + f_b * f_b <= PUPIL_R * PUPIL_R
        phase_re = jnp.where(inside, jnp.cos(phase_ref[...]), 0.0)
        phase_im = jnp.where(inside, jnp.sin(phase_ref[...]), 0.0)
        for s in range(sources_total):
            move_a = (FREQ - meta_ref[s // SRC_DEV, s % SRC_DEV, 0]) % FREQ
            move_b = (FREQ - meta_ref[s // SRC_DEV, s % SRC_DEV, 1]) % FREQ
            p_re = pltpu.roll(pltpu.roll(phase_re, move_a, 0), move_b, 1)
            p_im = pltpu.roll(pltpu.roll(phase_im, move_a, 0), move_b, 1)
            pupil_re[s] = p_re
            pupil_im[s] = p_im
            at = slice(s * FREQ, (s + 1) * FREQ)
            for part, value in (
                (slice(0, FREQ), p_re * spec_re - p_im * spec_im),
                (slice(FREQ, 2 * FREQ), p_re * spec_im + p_im * spec_re),
            ):
                top, low = split(value)
                amp_top[at, part] = top
                amp_low[at, part] = low
        damps[...] = jnp.zeros_like(damps)

    table = table_ref[...]
    intensity = jnp.zeros((table.shape[0], width), jnp.float32)
    weights = []
    for s in range(sources_total):
        weight = meta_ref[s // SRC_DEV, s % SRC_DEV, 2].astype(jnp.float32)
        weight = weight * (1.0 / (4.0 * sources_total))
        weights.append(weight)
        at = slice(s * FREQ, (s + 1) * FREQ)
        line = bdot(amp_top[at, :], line_top[...])
        line += bdot(amp_top[at, :], line_low[...]) + bdot(amp_low[at, :], line_top[...])
        re, im = line[:, :width].astype(jnp.bfloat16), line[:, width:].astype(jnp.bfloat16)
        field_re = bdot(table, jnp.concatenate([re, -im], axis=0))
        field_im = bdot(table, jnp.concatenate([im, re], axis=0))
        fields[s, :, :width] = field_re
        fields[s, :, width:] = field_im
        intensity += weight * (field_re * field_re + field_im * field_im)
    resist = 1.0 / (1.0 + jnp.exp(-steepness * (intensity - threshold)))
    resist_ref[0] = resist
    adjoint = 2.0 * (resist - target_ref[0].astype(jnp.float32)) * steepness
    adjoint = (adjoint * resist * (1.0 - resist)).astype(jnp.bfloat16).astype(jnp.float32)
    for s in range(sources_total):
        factor = 2.0 * weights[s] * adjoint
        d_re = (factor * fields[s, :, :width]).astype(jnp.bfloat16)
        d_im = (factor * fields[s, :, width:]).astype(jnp.bfloat16)
        b_re = bdot(table_t_ref[...], d_re)
        b_im = bdot(table_t_ref[...], d_im)
        at = slice(s * FREQ, (s + 1) * FREQ)
        dlines[at, :width] = b_re[:FREQ] + b_im[FREQ:]
        dlines[at, width:] = b_im[:FREQ] - b_re[FREQ:]
    d_top, d_low = split(dlines[...])
    damps[...] += (
        bdot_t(d_top, line_top[...]) + bdot_t(d_top, line_low[...]) + bdot_t(d_low, line_top[...])
    )

    @pl.when(step == pl.num_programs(0) - 1)
    def _():
        grad_re = jnp.zeros((FREQ, FREQ), jnp.float32)
        grad_im = jnp.zeros((FREQ, FREQ), jnp.float32)
        for s in range(sources_total):
            at = slice(s * FREQ, (s + 1) * FREQ)
            damp_re, damp_im = damps[at, :FREQ], damps[at, FREQ:]
            grad_re += pupil_re[s] * damp_re + pupil_im[s] * damp_im
            grad_im += pupil_re[s] * damp_im - pupil_im[s] * damp_re
        grad_ref[:, :FREQ] = scale_factor * grad_re
        grad_ref[:, FREQ:] = scale_factor * grad_im


def image_step(place, metas, half, rims, row_tables, phase, lines, table, table_t, target, rows):
    sources_total = SRC_DEV * metas.shape[0]
    scale_factor = 1.0 / (FREQ / 2 * math.sqrt(EXT_PX * TILE_PX))
    width = 256
    wide = 2 * FREQ

    def whole(*shape):
        return pl.BlockSpec(shape, lambda j, place, meta: (0,) * len(shape))

    grid_spec = pltpu.PrefetchScalarGridSpec(
        num_scalar_prefetch=2,
        grid=(TILE_PX // width,),
        in_specs=[
            whole(TILE_PX, wide),
            whole(2, HALO, wide),
            whole(wide, TILE_PX),
            whole(wide, TILE_PX),
            whole(wide, 2 * HALO),
            whole(wide, 2 * HALO),
            whole(FREQ, FREQ),
            pl.BlockSpec((wide, 2 * width), lambda j, place, meta: (0, j)),
            pl.BlockSpec((wide, 2 * width), lambda j, place, meta: (0, j)),
            pl.BlockSpec((rows, wide), lambda j, place, meta: (place[0], 0)),
            pl.BlockSpec((wide, rows), lambda j, place, meta: (0, place[0])),
            pl.BlockSpec((1, rows, width), lambda j, place, meta: (0, place[0], j)),
        ],
        out_specs=[
            pl.BlockSpec((1, rows, width), lambda j, place, meta: (0, 0, j)),
            whole(FREQ, wide),
        ],
        scratch_shapes=[
            pltpu.VMEM((sources_total, FREQ, FREQ), jnp.float32),
            pltpu.VMEM((sources_total, FREQ, FREQ), jnp.float32),
            pltpu.VMEM((sources_total * FREQ, wide), jnp.bfloat16),
            pltpu.VMEM((sources_total * FREQ, wide), jnp.bfloat16),
            pltpu.VMEM((sources_total, rows, 2 * width), jnp.float32),
            pltpu.VMEM((sources_total * FREQ, wide), jnp.float32),
            pltpu.VMEM((sources_total * FREQ, 2 * width), jnp.float32),
        ],
    )
    return pl.pallas_call(
        functools.partial(image_kernel, sources_total, scale_factor),
        grid_spec=grid_spec,
        out_shape=[
            jax.ShapeDtypeStruct((1, rows, TILE_PX), jnp.float32),
            jax.ShapeDtypeStruct((FREQ, wide), jnp.float32),
        ],
        compiler_params=pltpu.CompilerParams(vmem_limit_bytes=48 * 2**20),
        cost_estimate=pl.CostEstimate(flops=10**10, bytes_accessed=10**7, transcendentals=10**6),
    )(place, metas, half, rims, *row_tables, phase, *lines, table, table_t, target)


def exchange_back(tile_count, choice, grad, rim_table, own_table):
    held, sems = comm_scratch(tile_count)
    vmem = pl.BlockSpec(memory_space=pltpu.VMEM)
    return pl.pallas_call(
        functools.partial(back_kernel, tile_count),
        out_shape=jax.ShapeDtypeStruct(own_table.shape, jnp.float32),
        in_specs=[pl.BlockSpec(memory_space=pltpu.SMEM), vmem, vmem, vmem],
        out_specs=vmem,
        scratch_shapes=[
            held,
            pltpu.VMEM((lax.axis_size("src"), *grad.shape), jnp.float32),
            pltpu.VMEM((2 * FREQ, 2 * FREQ), jnp.float32),
            *sems,
        ],
        compiler_params=pltpu.CompilerParams(
            collective_id=1, has_side_effects=True, vmem_limit_bytes=16 * 2**20
        ),
        cost_estimate=pl.CostEstimate(flops=10**8, bytes_accessed=2**21, transcendentals=0),
    )(choice, grad, rim_table, own_table)


def per_device(mask_tiles, slot_pos, src_shift, src_weight, pupil_phase, target):
    tile_count = lax.axis_size("tile")
    my_src = lax.axis_index("src")
    rows = TILE_PX // lax.axis_size("src")
    col_cos, col_sin = np_tables(np.arange(TILE_PX), TILE_PX)
    row_cos, row_sin = np_tables(np.arange(EXT_PX), EXT_PX)
    col_both = np.concatenate([col_cos, col_sin], axis=1).astype(jnp.bfloat16)
    last_table = np.concatenate([col_cos.T, -col_sin.T], axis=0).astype(jnp.bfloat16)
    line_table = np.stack(
        [
            np.concatenate([col_cos.T, -col_sin.T], axis=0).reshape(2 * FREQ, -1, 256),
            np.concatenate([col_sin.T, col_cos.T], axis=0).reshape(2 * FREQ, -1, 256),
        ],
        axis=2,
    ).reshape(2 * FREQ, 2 * TILE_PX)
    row_both = np.concatenate([row_cos, row_sin], axis=1)
    row_own = np.ascontiguousarray(row_both[HALO : HALO + TILE_PX].T)
    row_rim = np.concatenate([row_both[:HALO], row_both[EXT_PX - HALO :]], axis=0).T
    row_tables = (*np_split(row_own), *np_split(np.ascontiguousarray(row_rim)))
    out_table = row_both[HALO : HALO + TILE_PX].astype(jnp.bfloat16)

    rims, metas, half_own = exchange_rims(
        tile_count, slot_pos, src_shift, src_weight, mask_tiles, col_both
    )
    place = jnp.full((1,), my_src, jnp.int32)
    resist, grad = image_step(
        place, metas, half_own, rims, row_tables, pupil_phase, np_split(line_table),
        out_table, np.ascontiguousarray(out_table.T), target, rows
    )
    row_array = jnp.asarray(row_both)
    own_table = lax.dynamic_slice_in_dim(row_array, HALO + my_src * rows, rows, 0)
    rim_start = jnp.where(my_src % 2 == 0, EXT_PX - HALO, 0)
    rim_table = lax.dynamic_slice_in_dim(row_array, rim_start, HALO, 0)
    back_rows = exchange_back(tile_count, slot_pos, grad, rim_table, own_table)
    step_rows = jnp.dot(
        back_rows.astype(jnp.bfloat16), last_table, preferred_element_type=jnp.float32
    )
    return (resist, (-learn_rate * step_rows)[None])


def solution(mesh):
    return jax.shard_map(
        per_device,
        mesh=mesh,
        in_specs=(P("tile", None, None), P(), P("src", None), P("src"), P(), P("tile", None, None)),
        out_specs=(P("tile", "src", None), P("tile", "src", None)),
        check_vma=False,
    )
```

time: 118 us -> 65.3 us (0.55)
  matrix products: 34.2 us -> 1.77 us
  other arithmetic: 23.7 us -> 0 us
  Pallas kernels: 35 us -> 54.9 us
  between operations: 18.2 us -> 0.78 us
  local copies, waits for them, and re-layouts: 6.18 us -> 7.5 us
    dot_general x14 -> x0, matrix products: 32.4 us -> none  [the longest x4 12.1 us: per_device(): fields = jnp.dot(my_table, stack, preferred_element_type=jnp.float32)]
    pallas_call x0 -> x1, Pallas kernels: none -> 19.7 us  [image_step(): pl.pallas_call(functools.partial(image_kernel, sources_total, scale_facto...]
    mul x7 -> x0, other arithmetic: 7.42 us -> none  [the longest x4 5.01 us: pupil_parts(): across[None, :] * across[None, :]]
    convert_element_type x3 -> x0, other arithmetic: 5.77 us -> none  [the longest x1 5.75 us: per_device(): adjoint = (2.0 * (resist_rows - my_target) * steepness * resist_rows * (1...]
    add x6 -> x0, other arithmetic: 4.96 us -> none  [the longest x4 2.32 us: per_device(): dline_re = blocks[:FREQ, :TILE_PX] + blocks[FREQ:, TILE_PX:]]
    unnamed x44 -> x30, local copies, waits for them, and re-layouts: 1.33 us -> 5.49 us
    reduce_sum x2 -> x0, other arithmetic: 2.73 us -> none  [the longest x1 1.44 us: per_device(): my_position = jnp.sum(jnp.where(slot_ids == my_slot, slot_pos, 0))]
    slice x4 -> x0, local copies, waits for them, and re-layouts: 2.48 us -> none  [the longest x1 1.21 us: per_device(): top = lines[s * FREQ:(s + 1) * FREQ]]
where the time goes in v1:
time: 65.3 us; the launch traced here: 65 us
  Pallas kernels  54.9 us (84%)
  local copies, waits for them, and re-layouts  7.5 us (11%)
  matrix products  1.77 us (3%)
  between operations  0.78 us (1%)
    pallas_call x1, Pallas kernels, image_step(): pl.pallas_call(functools.partial(image_kernel, sources_total, scale_facto...  19.7 us
    pallas_call x1, Pallas kernels, exchange_rims(): pl.pallas_call(functools.partial(rim_kernel, tile_count), out_shape=[jax....  18.2 us
    pallas_call x1, Pallas kernels, exchange_back(): pl.pallas_call(functools.partial(back_kernel, tile_count), out_shape=jax....  17 us
    unnamed x30, local copies, waits for them, and re-layouts  5.49 us
    dot_general x1, matrix products, per_device(): jnp.dot(back_rows.astype(jnp.bfloat16), last_table, preferred_element_typ...  1.77 us

profile of v1, /device:TPU:1, one launch (start us, length us, event | category | flops | bytes accessed | tf_op | source)
XLA Modules:
  0.0 65.0 jit_solution(1464154660806915377)
XLA Ops:
  0.6 0.0 copy-start.7
  0.6 0.0 copy-start.12
  0.7 0.0 copy-start.6
  0.7 0.9 %constant_dynamic-slice_fusion.1.rim_table = f32[64,256]{1,0:T(8,128)S(1)} fusion(f32[1152,256]{1,0:T(8,128)} %constant.60.clone, s32[]{:T(128)S(6)} %select_n.16), kind=kLoop, calls=%fused_computation.3 | loop fusion | bytes 131076 | tf_op jit(solution)/shard_map/dynamic_slice | solution.py:472
  1.6 1.1 %constant_dynamic-slice_fusion.own_table = f32[512,256]{1,0:T(8,128)S(1)} fusion(f32[1152,256]{1,0:T(8,128)} %constant.60.clone, s32[]{:T(128)S(6)} %select_n.17), kind=kLoop, calls=%fused_computation.2 | loop fusion | bytes 1048580 | tf_op jit(solution)/shard_map/dynamic_slice | solution.py:470
  2.7 0.0 copy-start
  2.7 1.6 %copy-done = bf16[1,1024,1024]{2,1,0:T(8,128)(2,1)S(1)} copy-done((bf16[1,1024,1024]{2,1,0:T(8,128)(2,1)S(1)}, bf16[1,1024,1024]{2,1,0:T(8,128)(2,1)}, u32[]{:S(2)}) %copy-start) | copy-done | bytes 2097176
  4.3 0.0 copy-start.1
  4.3 1.0 %copy-done.1 = bf16[1024,256]{1,0:T(8,128)(2,1)S(1)} copy-done((bf16[1024,256]{1,0:T(8,128)(2,1)S(1)}, bf16[1024,256]{1,0:T(8,128)(2,1)}, u32[]{:S(2)}) %copy-start.1) | copy-done | bytes 524312
  5.3 0.0 copy-start.2
  5.3 0.7 %copy-done.2 = s32[16]{0:T(128)S(1)} copy-done((s32[16]{0:T(128)S(1)}, s32[16]{0:T(128)}, u32[]{:S(2)}) %copy-start.2) | copy-done | bytes 88
  6.0 0.0 copy-start.4
  6.0 0.7 %copy-done.4 = s32[2,2]{1,0:T(2,128)S(1)} copy-done((s32[2,2]{1,0:T(2,128)S(1)}, s32[2,2]{1,0:T(2,128)}, u32[]{:S(2)}) %copy-start.4) | copy-done | bytes 40
  6.7 0.0 copy-start.5
  6.7 0.7 %copy-done.5 = s32[2]{0:T(128)S(1)} copy-done((s32[2]{0:T(128)S(1)}, s32[2]{0:T(128)}, u32[]{:S(2)}) %copy-start.5) | copy-done | bytes 32
  7.3 0.0 copy-start.8
  7.3 0.0 copy-start.9
  7.3 0.0 copy-start.10
  7.3 0.0 copy-start.11
  7.3 18.2 %shard_map.176 = (bf16[2,64,256]{2,1,0:T(8,128)(2,1)S(1)}, s32[2,8,128]{2,1,0:T(8,128)S(1)}, f32[1024,256]{1,0:T(8,128)S(1)}) custom-call(s32[16]{0:T(128)S(1)} %copy-done.2, s32[2,2]{1,0:T(2,128)S(1)} %copy-done.4, s32[2]{0:T(128)S(1)} %copy-done.5, bf16[1,1024,1024]{2,1,0:T(8,128)(2,1)S(1)} %copy-done, bf16[1024,256]{1,0:T(8,128)(2,1)S(1)} %copy-done.1), custom_call_target="tpu_custom_call" | custom-call | flops 600000000 | bytes 4194304 | tf_op jit(solution)/shard_map/pallas_call | solution.py:236
  25.5 0.0 copy-done.7
  25.5 0.0 copy-done.12
  25.6 0.0 copy-done.6
  25.6 0.0 copy-done.8
  25.6 0.0 copy-done.9
  25.6 0.0 copy-done.10
  25.6 0.0 copy-done.11
  25.6 0.0 copy-start.13
  25.6 0.8 %copy-done.13 = bf16[256,128]{1,0:T(8,128)(2,1)S(1)} copy-done((bf16[256,128]{1,0:T(8,128)(2,1)S(1)}, bf16[256,128]{1,0:T(8,128)(2,1)}, u32[]{:S(2)}) %copy-start.13) | copy-done | bytes 65560
  26.4 0.0 copy-start.3
  26.4 0.0 copy-start.14
  26.4 19.7 %shard_map.177 = (f32[1,512,1024]{2,1,0:T(8,128)}, f32[128,256]{1,0:T(8,128)S(1)}) custom-call(s32[1]{0:T(128)} %bitcast.place_ref, s32[2,8,128]{2,1,0:T(8,128)S(1)} %get-tuple-element.7.meta_ref, f32[1024,256]{1,0:T(8,128)S(1)} %get-tuple-element.8.half_ref, bf16[2,64,256]{2,1,0:T(8,128)(2,1)S(1)} %get-tuple-element.9.rims_ref, ...), custom_call_target="tpu_custom_call" | custom-call | flops 10000000000 | bytes 10000000 | tf_op jit(solution)/shard_map/pallas_call | solution.py:407
  46.2 0.0 copy-done.3
  46.2 17.0 %shard_map.178 = f32[512,256]{1,0:T(8,128)S(1)} custom-call(s32[16]{0:T(128)S(1)} %copy-done.3, f32[128,256]{1,0:T(8,128)S(1)} %get-tuple-element.11.grad_ref, f32[64,256]{1,0:T(8,128)S(1)} %constant_dynamic-slice_fusion.1.rim_table, f32[512,256]{1,0:T(8,128)S(1)} %constant_dynamic-slice_fusion.own_table), custom_call_target="tpu_custom_call" | custom-call | flops 100000000 | bytes 2097152 | tf_op jit(solution)/shard_map/pallas_call | solution.py:422
  63.2 0.0 copy-done.14
  63.2 1.8 %multiply_bitcast_fusion = f32[1,512,1024]{2,1,0:T(8,128)} fusion(bf16[256,1024]{1,0:T(8,128)(2,1)S(1)} %copy-done.14, f32[512,256]{1,0:T(8,128)S(1)} %shard_map.178), kind=kOutput, calls=%fused_computation | convolution fusion | flops 269090816 | bytes 3145728 | tf_op jit(solution)/shard_map/dot_general | solution.py:474
Async XLA Ops:
  0.6 24.9 %copy-start.7 = (bf16[256,2048]{1,0:T(8,128)(2,1)S(1)}, bf16[256,2048]{1,0:T(8,128)(2,1)}, u32[]{:S(2)}) copy-start(bf16[256,2048]{1,0:T(8,128)(2,1)} %constant.58.clone.line_low) | copy-start | bytes 3145732
  0.6 24.9 %copy-start.12 = (bf16[256,128]{1,0:T(8,128)(2,1)S(1)}, bf16[256,128]{1,0:T(8,128)(2,1)}, u32[]{:S(2)}) copy-start(bf16[256,128]{1,0:T(8,128)(2,1)} %constant.56.clone.rim_low) | copy-start | bytes 196612
  0.7 24.9 %copy-start.6 = (f32[128,128]{1,0:T(8,128)S(1)}, f32[128,128]{1,0:T(8,128)}, u32[]{:S(2)}) copy-start(f32[128,128]{1,0:T(8,128)} %phase_ref.1) | copy-start | bytes 196612
  2.7 1.6 %copy-start = (bf16[1,1024,1024]{2,1,0:T(8,128)(2,1)S(1)}, bf16[1,1024,1024]{2,1,0:T(8,128)(2,1)}, u32[]{:S(2)}) copy-start(bf16[1,1024,1024]{2,1,0:T(8,128)(2,1)} %mask_ref.1) | copy-start | bytes 6291460
  4.3 1.0 %copy-start.1 = (bf16[1024,256]{1,0:T(8,128)(2,1)S(1)}, bf16[1024,256]{1,0:T(8,128)(2,1)}, u32[]{:S(2)}) copy-start(bf16[1024,256]{1,0:T(8,128)(2,1)} %constant.52.clone.table_ref) | copy-start | bytes 1572868
  5.3 0.7 %copy-start.2 = (s32[16]{0:T(128)S(1)}, s32[16]{0:T(128)}, u32[]{:S(2)}) copy-start(s32[16]{0:T(128)} %pos_ref.3) | copy-start | bytes 196
  6.0 0.7 %copy-start.4 = (s32[2,2]{1,0:T(2,128)S(1)}, s32[2,2]{1,0:T(2,128)}, u32[]{:S(2)}) copy-start(s32[2,2]{1,0:T(2,128)} %shift_ref.1) | copy-start | bytes 52
  6.7 0.7 %copy-start.5 = (s32[2]{0:T(128)S(1)}, s32[2]{0:T(128)}, u32[]{:S(2)}) copy-start(s32[2]{0:T(128)} %weight_ref.1) | copy-start | bytes 28
  7.3 18.2 %copy-start.8 = (bf16[256,2048]{1,0:T(8,128)(2,1)S(1)}, bf16[256,2048]{1,0:T(8,128)(2,1)}, u32[]{:S(2)}) copy-start(bf16[256,2048]{1,0:T(8,128)(2,1)} %constant.57.clone.line_top) | copy-start | bytes 3145732
  7.3 18.2 %copy-start.9 = (bf16[1024,256]{1,0:T(8,128)(2,1)S(1)}, bf16[1024,256]{1,0:T(8,128)(2,1)}, u32[]{:S(2)}) copy-start(bf16[1024,256]{1,0:T(8,128)(2,1)} %constant.59.clone.table_ref) | copy-start | bytes 1572868
  7.3 18.3 %copy-start.10 = (bf16[256,1024]{1,0:T(8,128)(2,1)S(1)}, bf16[256,1024]{1,0:T(8,128)(2,1)}, u32[]{:S(2)}) copy-start(bf16[256,1024]{1,0:T(8,128)(2,1)} %constant.54.clone.own_low) | copy-start | bytes 1572868
  7.3 18.3 %copy-start.11 = (bf16[256,1024]{1,0:T(8,128)(2,1)S(1)}, bf16[256,1024]{1,0:T(8,128)(2,1)}, u32[]{:S(2)}) copy-start(bf16[256,1024]{1,0:T(8,128)(2,1)} %constant.53.clone.own_top.table_t_ref) | copy-start | bytes 1572868
  25.6 0.8 %copy-start.13 = (bf16[256,128]{1,0:T(8,128)(2,1)S(1)}, bf16[256,128]{1,0:T(8,128)(2,1)}, u32[]{:S(2)}) copy-start(bf16[256,128]{1,0:T(8,128)(2,1)} %constant.55.clone.rim_top) | copy-start | bytes 196612
  26.4 19.7 %copy-start.3 = (s32[16]{0:T(128)S(1)}, s32[16]{0:T(128)}, u32[]{:S(2)}) copy-start(s32[16]{0:T(128)} %pos_ref.3) | copy-start | bytes 196
  26.4 36.8 %copy-start.14 = (bf16[256,1024]{1,0:T(8,128)(2,1)S(1)}, bf16[256,1024]{1,0:T(8,128)(2,1)}, u32[]{:S(2)}) copy-start(bf16[256,1024]{1,0:T(8,128)(2,1)} %constant.61.clone) | copy-start | bytes 1572868

commit v2 on v1

--- a/solution.py
+++ b/solution.py
@@ -39,6 +39,12 @@
     return low, tile_count // low
 
 
+def low_peers(low, my_low):
+    if low == 1:
+        return []
+    return [(my_low + 2) % 4, my_low + 1 - 2 * (my_low % 2)]
+
+
 def greet(tile_count):
     low, high = group_sizes(tile_count)
     tile = lax.axis_index("tile")
@@ -49,13 +55,14 @@
     for k in range(1, high):
         peer = ((my_high + k) % high) * low + my_low
         pl.semaphore_signal(barrier, inc=1, device_id={"tile": peer}, device_id_type=MESH)
-    for j in range(1, low):
-        peer = my_high * low + (my_low + j) % low
+    near = low_peers(low, my_low)
+    for other in near:
+        peer = my_high * low + other
         pl.semaphore_signal(barrier, inc=1, device_id={"tile": peer}, device_id_type=MESH)
     for k in range(1, src_count):
         peer = (src + k) % src_count
         pl.semaphore_signal(barrier, inc=1, device_id={"src": peer}, device_id_type=MESH)
-    pl.semaphore_wait(barrier, high - 1 + low - 1 + src_count - 1)
+    pl.semaphore_wait(barrier, high - 1 + len(near) + src_count - 1)
 
 
 def start_high(tile_count, held, sends, recvs):
@@ -82,20 +89,33 @@
     low, high = group_sizes(tile_count)
     tile = lax.axis_index("tile")
     my_high, my_low = tile // low, tile % low
-    copies = []
-    for j in range(1, low):
-        peer = my_high * low + (my_low + j) % low
-        copy = pltpu.make_async_remote_copy(
-            src_ref=held.at[my_low],
-            dst_ref=held.at[my_low],
-            send_sem=sends.at[j - 1],
-            recv_sem=recvs.at[j - 1],
-            device_id={"tile": peer},
+
+    def copy_of(which, block, other):
+        return pltpu.make_async_remote_copy(
+            src_ref=held.at[block],
+            dst_ref=held.at[block],
+            send_sem=sends.at[which],
+            recv_sem=recvs.at[which],
+            device_id={"tile": my_high * low + other},
             device_id_type=MESH,
         )
-        copy.start()
-        copies.append(copy)
-    return copies
+
+    if low == 1:
+        return lambda: None
+    far, beside = low_peers(low, my_low)
+    first = copy_of(0, my_low, far)
+    first.start()
+    second = copy_of(1, my_low, beside)
+    second.start()
+
+    def finish():
+        first.wait()
+        third = copy_of(2, far, beside)
+        third.start()
+        second.wait()
+        third.wait()
+
+    return finish
 
 
 def pick(tile_count, held, pos_ref):
@@ -131,8 +151,8 @@
 
 
 def rim_kernel(
-    tile_count, pos_ref, shift_ref, weight_ref, mask_ref, table_ref, rims_out, meta_out, half_out,
-    held, rims, meta_held, send_a, recv_a, send_b, recv_b, send_s, recv_s, send_r, recv_r
+    tile_count, pos_ref, shift_ref, weight_ref, mask_ref, table_ref, own_top, own_low, phase_ref,
+    rims_out, meta_out, spec_out, pupil_out, held, rims, meta_held, send_a, recv_a, send_b, recv_b, send_s, recv_s, send_r, recv_r
 ):
     low, high = group_sizes(tile_count)
     tile = lax.axis_index("tile")
@@ -156,18 +176,15 @@
     meta_copies = start_src(meta_held, send_s, recv_s)
     for copy in high_copies:
         copy.wait()
-    low_copies = start_low(tile_count, held, send_b, recv_b)
-
-    def transform(i, carry):
-        at = pl.ds(pl.multiple_of(i * 256, 256), 256)
-        half_out[at, :] = jnp.dot(
-            mask_ref[0, at, :], table_ref[...], preferred_element_type=jnp.float32
-        )
-        return carry
-
-    lax.fori_loop(0, TILE_PX // 256, transform, 0)
-    for copy in low_copies:
-        copy.wait()
+    finish_low = start_low(tile_count, held, send_b, recv_b)
+    spec = jnp.zeros((2 * FREQ, 2 * FREQ), jnp.float32)
+    for i in range(TILE_PX // 256):
+        at = slice(i * 256, (i + 1) * 256)
+        half_top, half_low = split(bdot(mask_ref[0, at, :], table_ref[...]))
+        spec += bdot(own_top[:, at], half_top)
+        spec += bdot(own_top[:, at], half_low) + bdot(own_low[:, at], half_top)
+    spec_out[...] = spec
+    finish_low()
     rims[side] = pick(tile_count, held, pos_ref).astype(jnp.bfloat16)
     rim_copy = pltpu.make_async_remote_copy(
         src_ref=rims.at[side],
@@ -178,6 +195,11 @@
         device_id_type=MESH,
     )
     rim_copy.start()
+    f_a = lax.broadcasted_iota(jnp.int32, (FREQ, FREQ), 0) - FREQ // 2
+    f_b = lax.broadcasted_iota(jnp.int32, (FREQ, FREQ), 1) - FREQ // 2
+    inside = f_a * f_a + f_b * f_b <= PUPIL_R * PUPIL_R
+    pupil_out[0] = jnp.where(inside, jnp.cos(phase_ref[...]), 0.0)
+    pupil_out[1] = jnp.where(inside, jnp.sin(phase_ref[...]), 0.0)
     for copy in meta_copies:
         copy.wait()
     meta_out[...] = meta_held[...]
@@ -186,7 +208,7 @@
 
 
 def back_kernel(
-    tile_count, pos_ref, grad_ref, rim_table, own_table, out_ref,
+    tile_count, pos_ref, grad_ref, row_table, out_ref,
     held, grads, total, send_a, recv_a, send_b, recv_b, send_s, recv_s
 ):
     low, high = group_sizes(tile_count)
@@ -203,16 +225,17 @@
     total[:FREQ, :] = both
     total[FREQ:, :FREQ] = -both[:, FREQ:]
     total[FREQ:, FREQ:] = both[:, :FREQ]
-    rim_back = fdot(rim_table[...], total[...], HIGHEST)
+    rim_at = pl.multiple_of((1 - src % 2) * (EXT_PX - HALO), HALO)
+    rim_back = fdot(row_table[pl.ds(rim_at, HALO), :], total[...], HIGHEST)
     held[tile % low, tile // low] = rim_back.astype(jnp.bfloat16)
     high_copies = start_high(tile_count, held, send_a, recv_a)
-    out_ref[...] = fdot(own_table[...], total[...], HIGHEST)
+    rows = out_ref.shape[0]
+    own_at = pl.multiple_of(HALO + src * rows, HALO)
+    out_ref[...] = fdot(row_table[pl.ds(own_at, rows), :], total[...], HIGHEST)
     for copy in high_copies:
         copy.wait()
-    for copy in start_low(tile_count, held, send_b, recv_b):
-        copy.wait()
+    start_low(tile_count, held, send_b, recv_b)()
     block = pick(tile_count, held, pos_ref)
-    rows = out_ref.shape[0]
     first = jnp.where(src == 0, 1.0, 0.0)
     last = jnp.where(src == src_count - 1, 1.0, 0.0)
     out_ref[:HALO, :] += first * block
@@ -227,7 +250,7 @@
     return held, sems
 
 
-def exchange_rims(tile_count, slot_pos, src_shift, src_weight, mask_tiles, table):
+def exchange_rims(tile_count, slot_pos, src_shift, src_weight, mask_tiles, *tables):
     held, sems = comm_scratch(tile_count)
     block = (HALO, 2 * FREQ)
     metas = (lax.axis_size("src"), 8, 128)
@@ -238,10 +261,11 @@
         out_shape=[
             jax.ShapeDtypeStruct((2, *block), jnp.bfloat16),
             jax.ShapeDtypeStruct(metas, jnp.int32),
-            jax.ShapeDtypeStruct((TILE_PX, 2 * FREQ), jnp.float32),
-        ],
-        in_specs=[smem, smem, smem, vmem, vmem],
-        out_specs=[vmem] * 3,
+            jax.ShapeDtypeStruct((2 * FREQ, 2 * FREQ), jnp.float32),
+            jax.ShapeDtypeStruct((2, FREQ, FREQ), jnp.float32),
+        ],
+        in_specs=[smem, smem, smem, vmem] + [vmem] * len(tables),
+        out_specs=[vmem] * 4,
         scratch_shapes=[
             held,
             pltpu.VMEM((2, *block), jnp.bfloat16),
@@ -251,10 +275,10 @@
             pltpu.SemaphoreType.DMA((1,)),
         ],
         compiler_params=pltpu.CompilerParams(
-            collective_id=0, has_side_effects=True, vmem_limit_bytes=24 * 2**20
+            collective_id=0, has_side_effects=True, vmem_limit_bytes=56 * 2**20
         ),
         cost_estimate=pl.CostEstimate(flops=6 * 10**8, bytes_accessed=2**22, transcendentals=0),
-    )(slot_pos, src_shift, src_weight, mask_tiles, table)
+    )(slot_pos, src_shift, src_weight, mask_tiles, *tables)
 
 
 def split(value):
@@ -279,7 +303,7 @@
 
 def image_kernel(
     sources_total, scale_factor, place_ref, meta_ref,
-    half_ref, rims_ref, own_top, own_low, rim_top, rim_low, phase_ref, line_top, line_low,
+    spec_ref, rims_ref, rim_top, rim_low, phase_ref, line_top, line_low,
     table_ref, table_t_ref, target_ref, resist_ref, grad_ref,
     pupil_re, pupil_im, amp_top, amp_low, fields, damps, dlines
 ):
@@ -288,18 +312,11 @@
 
     @pl.when(step == 0)
     def _():
-        half_top, half_low = split(half_ref[...])
-        spec4 = bdot(own_top[...], half_top)
-        spec4 += bdot(own_top[...], half_low) + bdot(own_low[...], half_top)
         rims = rims_ref[...].reshape(2 * HALO, 2 * FREQ)
-        spec4 += bdot(rim_top[...], rims) + bdot(rim_low[...], rims)
+        spec4 = spec_ref[...] + bdot(rim_top[...], rims) + bdot(rim_low[...], rims)
         spec_re = scale_factor * (spec4[:FREQ, :FREQ] - spec4[FREQ:, FREQ:])
         spec_im = -scale_factor * (spec4[:FREQ, FREQ:] + spec4[FREQ:, :FREQ])
-        f_a = lax.broadcasted_iota(jnp.int32, (FREQ, FREQ), 0) - FREQ // 2
-        f_b = lax.broadcasted_iota(jnp.int32, (FREQ, FREQ), 1) - FREQ // 2
-        inside = f_a * f_a + f_b * f_b <= PUPIL_R * PUPIL_R
-        phase_re = jnp.where(inside, jnp.cos(phase_ref[...]), 0.0)
-        phase_im = jnp.where(inside, jnp.sin(phase_ref[...]), 0.0)
+        phase_re, phase_im = phase_ref[0], phase_ref[1]
         for s in range(sources_total):
             move_a = (FREQ - meta_ref[s // SRC_DEV, s % SRC_DEV, 0]) % FREQ
             move_b = (FREQ - meta_ref[s // SRC_DEV, s % SRC_DEV, 1]) % FREQ
@@ -344,12 +361,9 @@
         b_re = bdot(table_t_ref[...], d_re)
         b_im = bdot(table_t_ref[...], d_im)
         at = slice(s * FREQ, (s + 1) * FREQ)
-        dlines[at, :width] = b_re[:FREQ] + b_im[FREQ:]
-        dlines[at, width:] = b_im[:FREQ] - b_re[FREQ:]
-    d_top, d_low = split(dlines[...])
-    damps[...] += (
-        bdot_t(d_top, line_top[...]) + bdot_t(d_top, line_low[...]) + bdot_t(d_low, line_top[...])
-    )
+        dlines[at, :width] = (b_re[:FREQ] + b_im[FREQ:]).astype(jnp.bfloat16)
+        dlines[at, width:] = (b_im[:FREQ] - b_re[FREQ:]).astype(jnp.bfloat16)
+    damps[...] += bdot_t(dlines[...], line_top[...])
 
     @pl.when(step == pl.num_programs(0) - 1)
     def _():
@@ -364,7 +378,7 @@
         grad_ref[:, FREQ:] = scale_factor * grad_im
 
 
-def image_step(place, metas, half, rims, row_tables, phase, lines, table, table_t, target, rows):
+def image_step(place, metas, spec, rims, row_tables, phase, lines, table, table_t, target, rows):
     sources_total = SRC_DEV * metas.shape[0]
     scale_factor = 1.0 / (FREQ / 2 * math.sqrt(EXT_PX * TILE_PX))
     width = 256
@@ -377,13 +391,11 @@
         num_scalar_prefetch=2,
         grid=(TILE_PX // width,),
         in_specs=[
-            whole(TILE_PX, wide),
+            whole(wide, wide),
             whole(2, HALO, wide),
-            whole(wide, TILE_PX),
-            whole(wide, TILE_PX),
             whole(wide, 2 * HALO),
             whole(wide, 2 * HALO),
-            whole(FREQ, FREQ),
+            whole(2, FREQ, FREQ),
             pl.BlockSpec((wide, 2 * width), lambda j, place, meta: (0, j)),
             pl.BlockSpec((wide, 2 * width), lambda j, place, meta: (0, j)),
             pl.BlockSpec((rows, wide), lambda j, place, meta: (place[0], 0)),
@@ -401,7 +413,7 @@
             pltpu.VMEM((sources_total * FREQ, wide), jnp.bfloat16),
             pltpu.VMEM((sources_total, rows, 2 * width), jnp.float32),
             pltpu.VMEM((sources_total * FREQ, wide), jnp.float32),
-            pltpu.VMEM((sources_total * FREQ, 2 * width), jnp.float32),
+            pltpu.VMEM((sources_total * FREQ, 2 * width), jnp.bfloat16),
         ],
     )
     return pl.pallas_call(
@@ -413,16 +425,16 @@
         ],
         compiler_params=pltpu.CompilerParams(vmem_limit_bytes=48 * 2**20),
         cost_estimate=pl.CostEstimate(flops=10**10, bytes_accessed=10**7, transcendentals=10**6),
-    )(place, metas, half, rims, *row_tables, phase, *lines, table, table_t, target)
-
-
-def exchange_back(tile_count, choice, grad, rim_table, own_table):
+    )(place, metas, spec, rims, *row_tables, phase, *lines, table, table_t, target)
+
+
+def exchange_back(tile_count, slot_pos, grad, row_table, rows):
     held, sems = comm_scratch(tile_count)
     vmem = pl.BlockSpec(memory_space=pltpu.VMEM)
     return pl.pallas_call(
         functools.partial(back_kernel, tile_count),
-        out_shape=jax.ShapeDtypeStruct(own_table.shape, jnp.float32),
-        in_specs=[pl.BlockSpec(memory_space=pltpu.SMEM), vmem, vmem, vmem],
+        out_shape=jax.ShapeDtypeStruct((rows, 2 * FREQ), jnp.float32),
+        in_specs=[pl.BlockSpec(memory_space=pltpu.SMEM), vmem, vmem],
         out_specs=vmem,
         scratch_shapes=[
             held,
@@ -431,10 +443,10 @@
             *sems,
         ],
         compiler_params=pltpu.CompilerParams(
-            collective_id=1, has_side_effects=True, vmem_limit_bytes=16 * 2**20
+            collective_id=1, has_side_effects=True, vmem_limit_bytes=56 * 2**20
         ),
         cost_estimate=pl.CostEstimate(flops=10**8, bytes_accessed=2**21, transcendentals=0),
-    )(choice, grad, rim_table, own_table)
+    )(slot_pos, grad, row_table)
 
 
 def per_device(mask_tiles, slot_pos, src_shift, src_weight, pupil_phase, target):
@@ -455,22 +467,19 @@
     row_both = np.concatenate([row_cos, row_sin], axis=1)
     row_own = np.ascontiguousarray(row_both[HALO : HALO + TILE_PX].T)
     row_rim = np.concatenate([row_both[:HALO], row_both[EXT_PX - HALO :]], axis=0).T
-    row_tables = (*np_split(row_own), *np_split(np.ascontiguousarray(row_rim)))
+    rim_tables = np_split(np.ascontiguousarray(row_rim))
     out_table = row_both[HALO : HALO + TILE_PX].astype(jnp.bfloat16)
 
-    rims, metas, half_own = exchange_rims(
-        tile_count, slot_pos, src_shift, src_weight, mask_tiles, col_both
+    rims, metas, spec_own, pupil = exchange_rims(
+        tile_count, slot_pos, src_shift, src_weight, mask_tiles, col_both,
+        *np_split(row_own), pupil_phase
     )
     place = jnp.full((1,), my_src, jnp.int32)
     resist, grad = image_step(
-        place, metas, half_own, rims, row_tables, pupil_phase, np_split(line_table),
+        place, metas, spec_own, rims, rim_tables, pupil, np_split(line_table),
         out_table, np.ascontiguousarray(out_table.T), target, rows
     )
-    row_array = jnp.asarray(row_both)
-    own_table = lax.dynamic_slice_in_dim(row_array, HALO + my_src * rows, rows, 0)
-    rim_start = jnp.where(my_src % 2 == 0, EXT_PX - HALO, 0)
-    rim_table = lax.dynamic_slice_in_dim(row_array, rim_start, HALO, 0)
-    back_rows = exchange_back(tile_count, slot_pos, grad, rim_table, own_table)
+    back_rows = exchange_back(tile_count, slot_pos, grad, row_both, rows)
     step_rows = jnp.dot(
         back_rows.astype(jnp.bfloat16), last_table, preferred_element_type=jnp.float32
     )

time: 65.3 us -> 64.6 us (0.989)
  Pallas kernels: 54.9 us -> 53.3 us
  matrix products: 1.77 us -> 2.8 us
    pallas_call x1, Pallas kernels: 19.7 us -> 15.3 us  [image_step(): pl.pallas_call(functools.partial(image_kernel, sources_total, scale_facto...]
    dynamic_slice x2 -> x0, local copies, waits for them, and re-layouts: 2.01 us -> none  [the longest x1 1.08 us: per_device(): lax.dynamic_slice_in_dim(row_array, HALO + my_src * rows, rows, 0)]
    pallas_call x1, Pallas kernels: 18.2 us -> 20.1 us  [exchange_rims(): pl.pallas_call(functools.partial(rim_kernel, tile_count), out_shape=[jax....]
    unnamed x30 -> x26, local copies, waits for them, and re-layouts: 5.49 us -> 7.17 us
    dot_general x1, matrix products: 1.77 us -> 2.8 us  [per_device(): jnp.dot(back_rows.astype(jnp.bfloat16), last_table, preferred_element_typ...]
    pallas_call x1, Pallas kernels: 17 us -> 18 us  [exchange_back(): pl.pallas_call(functools.partial(back_kernel, tile_count), out_shape=jax....]
where the time goes in v2:
time: 64.6 us; the launch traced here: 64 us
  Pallas kernels  53.3 us (83%)
  local copies, waits for them, and re-layouts  7.17 us (11%)
  matrix products  2.8 us (4%)
  between operations  0.74 us (1%)
    pallas_call x1, Pallas kernels, exchange_rims(): pl.pallas_call(functools.partial(rim_kernel, tile_count), out_shape=[jax....  20.1 us
    pallas_call x1, Pallas kernels, exchange_back(): pl.pallas_call(functools.partial(back_kernel, tile_count), out_shape=jax....  18 us
    pallas_call x1, Pallas kernels, image_step(): pl.pallas_call(functools.partial(image_kernel, sources_total, scale_facto...  15.3 us
    unnamed x26, local copies, waits for them, and re-layouts  7.17 us
    dot_general x1, matrix products, per_device(): jnp.dot(back_rows.astype(jnp.bfloat16), last_table, preferred_element_typ...  2.8 us

profile of v2, /device:TPU:1, one launch (start us, length us, event | category | flops | bytes accessed | tf_op | source)
XLA Modules:
  0.0 64.0 jit_solution(2277118226861665323)
XLA Ops:
  0.6 0.0 copy-start
  0.6 0.0 copy-start.10
  0.7 0.0 copy-start.2
  0.7 0.0 copy-start.7
  0.7 20.1 %shard_map.176 = (bf16[2,64,256]{2,1,0:T(8,128)(2,1)}, s32[2,8,128]{2,1,0:T(8,128)}, f32[256,256]{1,0:T(8,128)}, f32[2,128,128]{2,1,0:T(8,128)}) custom-call(s32[16]{0:T(128)} %pos_ref.3, s32[2,2]{1,0:T(2,128)} %shift_ref.1, s32[2]{0:T(128)} %weight_ref.1, bf16[1,1024,1024]{2,1,0:T(8,128)(2,1)} %mask_ref.1, bf16[1024,256]{1,0:T(8,128)(2,1)} %constant.28.clone.table_ref, ...), custom_call_target="tpu_custom_call" | custom-call | flops 600000000 | bytes 4194304 | tf_op jit(solution)/shard_map/pallas_call | solution.py:259
  20.7 0.0 copy-done
  20.8 0.0 copy-done.10
  20.8 0.0 copy-done.2
  20.8 0.0 copy-done.7
  20.8 0.0 copy-start.3
  20.8 0.9 %copy-done.3 = f32[256,256]{1,0:T(8,128)S(1)} copy-done((f32[256,256]{1,0:T(8,128)S(1)}, f32[256,256]{1,0:T(8,128)}, u32[]{:S(2)}) %copy-start.3) | copy-done | bytes 262168
  21.7 0.0 copy-start.4
  21.7 0.9 %copy-done.4 = f32[2,128,128]{2,1,0:T(8,128)S(1)} copy-done((f32[2,128,128]{2,1,0:T(8,128)S(1)}, f32[2,128,128]{2,1,0:T(8,128)}, u32[]{:S(2)}) %copy-start.4) | copy-done | bytes 131096
  22.6 0.0 copy-start.5
  22.6 0.8 %copy-done.5 = bf16[2,64,256]{2,1,0:T(8,128)(2,1)S(1)} copy-done((bf16[2,64,256]{2,1,0:T(8,128)(2,1)S(1)}, bf16[2,64,256]{2,1,0:T(8,128)(2,1)}, u32[]{:S(2)}) %copy-start.5) | copy-done | bytes 65560
  23.5 0.0 copy-start.6
  23.5 0.7 %copy-done.6 = s32[2,8,128]{2,1,0:T(8,128)S(1)} copy-done((s32[2,8,128]{2,1,0:T(8,128)S(1)}, s32[2,8,128]{2,1,0:T(8,128)}, u32[]{:S(2)}) %copy-start.6) | copy-done | bytes 8216
  24.2 0.0 copy-start.8
  24.2 1.2 %copy-done.8 = bf16[256,2048]{1,0:T(8,128)(2,1)S(1)} copy-done((bf16[256,2048]{1,0:T(8,128)(2,1)S(1)}, bf16[256,2048]{1,0:T(8,128)(2,1)}, u32[]{:S(2)}) %copy-start.8) | copy-done | bytes 1048600
  25.4 0.0 copy-start.9
  25.4 1.0 %copy-done.9 = bf16[1024,256]{1,0:T(8,128)(2,1)S(1)} copy-done((bf16[1024,256]{1,0:T(8,128)(2,1)S(1)}, bf16[1024,256]{1,0:T(8,128)(2,1)}, u32[]{:S(2)}) %copy-start.9) | copy-done | bytes 524312
  26.4 0.0 copy-start.11
  26.4 0.8 %copy-done.11 = bf16[256,128]{1,0:T(8,128)(2,1)S(1)} copy-done((bf16[256,128]{1,0:T(8,128)(2,1)S(1)}, bf16[256,128]{1,0:T(8,128)(2,1)}, u32[]{:S(2)}) %copy-start.11) | copy-done | bytes 65560
  27.3 15.3 %shard_map.177 = (f32[1,512,1024]{2,1,0:T(8,128)}, f32[128,256]{1,0:T(8,128)S(1)}) custom-call(s32[1]{0:T(128)} %bitcast.place_ref, s32[2,8,128]{2,1,0:T(8,128)S(1)} %copy-done.6, f32[256,256]{1,0:T(8,128)S(1)} %copy-done.3, bf16[2,64,256]{2,1,0:T(8,128)(2,1)S(1)} %copy-done.5, bf16[256,128]{1,0:T(8,128)(2,1)S(1)} %copy-done.11, ...), custom_call_target="tpu_custom_call" | custom-call | flops 10000000000 | bytes 10000000 | tf_op jit(solution)/shard_map/pallas_call | solution.py:419
  42.5 0.0 copy-start.1
  42.5 0.7 %copy-done.1 = f32[128,256]{1,0:T(8,128)} copy-done((f32[128,256]{1,0:T(8,128)}, f32[128,256]{1,0:T(8,128)S(1)}, u32[]{:S(2)}) %copy-start.1) | copy-done | bytes 131096
  43.2 0.0 copy-start.12
  43.2 18.0 %shard_map.178 = f32[512,256]{1,0:T(8,128)} custom-call(s32[16]{0:T(128)} %pos_ref.3, f32[128,256]{1,0:T(8,128)} %copy-done.1, f32[1152,256]{1,0:T(8,128)} %constant.36.clone.row_table), custom_call_target="tpu_custom_call" | custom-call | flops 100000000 | bytes 2097152 | tf_op jit(solution)/shard_map/pallas_call | solution.py:434
  61.2 0.0 copy-done.12
  61.2 2.8 %multiply_bitcast_fusion = f32[1,512,1024]{2,1,0:T(8,128)} fusion(bf16[256,1024]{1,0:T(8,128)(2,1)S(1)} %copy-done.12, f32[512,256]{1,0:T(8,128)} %shard_map.178), kind=kOutput, calls=%fused_computation | convolution fusion | flops 269090816 | bytes 3145728 | tf_op jit(solution)/shard_map/dot_general | solution.py:483
Async XLA Ops:
  0.6 20.1 %copy-start = (bf16[256,1024]{1,0:T(8,128)(2,1)S(1)}, bf16[256,1024]{1,0:T(8,128)(2,1)}, u32[]{:S(2)}) copy-start(bf16[256,1024]{1,0:T(8,128)(2,1)} %constant.29.clone.own_top.table_t_ref) | copy-start | bytes 1572868
  0.6 20.1 %copy-start.10 = (bf16[256,128]{1,0:T(8,128)(2,1)S(1)}, bf16[256,128]{1,0:T(8,128)(2,1)}, u32[]{:S(2)}) copy-start(bf16[256,128]{1,0:T(8,128)(2,1)} %constant.32.clone.rim_low) | copy-start | bytes 196612
  0.7 20.1 %copy-start.2 = (bf16[1,1024,1024]{2,1,0:T(8,128)(2,1)S(1)}, bf16[1,1024,1024]{2,1,0:T(8,128)(2,1)}, u32[]{:S(2)}) copy-start(bf16[1,1024,1024]{2,1,0:T(8,128)(2,1)} %target_ref.1) | copy-start | bytes 6291460
  0.7 20.1 %copy-start.7 = (bf16[256,2048]{1,0:T(8,128)(2,1)S(1)}, bf16[256,2048]{1,0:T(8,128)(2,1)}, u32[]{:S(2)}) copy-start(bf16[256,2048]{1,0:T(8,128)(2,1)} %constant.34.clone.line_low) | copy-start | bytes 3145732
  20.8 1.0 %copy-start.3 = (f32[256,256]{1,0:T(8,128)S(1)}, f32[256,256]{1,0:T(8,128)}, u32[]{:S(2)}) copy-start(f32[256,256]{1,0:T(8,128)} %get-tuple-element.9.spec_ref) | copy-start | bytes 786436
  21.7 0.9 %copy-start.4 = (f32[2,128,128]{2,1,0:T(8,128)S(1)}, f32[2,128,128]{2,1,0:T(8,128)}, u32[]{:S(2)}) copy-start(f32[2,128,128]{2,1,0:T(8,128)} %get-tuple-element.11.phase_ref) | copy-start | bytes 393220
  22.6 0.8 %copy-start.5 = (bf16[2,64,256]{2,1,0:T(8,128)(2,1)S(1)}, bf16[2,64,256]{2,1,0:T(8,128)(2,1)}, u32[]{:S(2)}) copy-start(bf16[2,64,256]{2,1,0:T(8,128)(2,1)} %get-tuple-element.10.rims_ref) | copy-start | bytes 196612
  23.5 0.7 %copy-start.6 = (s32[2,8,128]{2,1,0:T(8,128)S(1)}, s32[2,8,128]{2,1,0:T(8,128)}, u32[]{:S(2)}) copy-start(s32[2,8,128]{2,1,0:T(8,128)} %get-tuple-element.8.meta_ref) | copy-start | bytes 24580
  24.2 1.2 %copy-start.8 = (bf16[256,2048]{1,0:T(8,128)(2,1)S(1)}, bf16[256,2048]{1,0:T(8,128)(2,1)}, u32[]{:S(2)}) copy-start(bf16[256,2048]{1,0:T(8,128)(2,1)} %constant.33.clone.line_top) | copy-start | bytes 3145732
  25.4 1.0 %copy-start.9 = (bf16[1024,256]{1,0:T(8,128)(2,1)S(1)}, bf16[1024,256]{1,0:T(8,128)(2,1)}, u32[]{:S(2)}) copy-start(bf16[1024,256]{1,0:T(8,128)(2,1)} %constant.35.clone.table_ref) | copy-start | bytes 1572868
  26.4 0.8 %copy-start.11 = (bf16[256,128]{1,0:T(8,128)(2,1)S(1)}, bf16[256,128]{1,0:T(8,128)(2,1)}, u32[]{:S(2)}) copy-start(bf16[256,128]{1,0:T(8,128)(2,1)} %constant.31.clone.rim_top) | copy-start | bytes 196612
  42.5 0.7 %copy-start.1 = (f32[128,256]{1,0:T(8,128)}, f32[128,256]{1,0:T(8,128)S(1)}, u32[]{:S(2)}) copy-start(f32[128,256]{1,0:T(8,128)S(1)} %get-tuple-element.13.grad_ref) | copy-start | bytes 393220
  43.2 18.0 %copy-start.12 = (bf16[256,1024]{1,0:T(8,128)(2,1)S(1)}, bf16[256,1024]{1,0:T(8,128)(2,1)}, u32[]{:S(2)}) copy-start(bf16[256,1024]{1,0:T(8,128)(2,1)} %constant.37.clone) | copy-start | bytes 1572868

commit v3 on v2

--- a/solution.py
+++ b/solution.py
@@ -151,13 +151,24 @@
 
 
 def rim_kernel(
-    tile_count, pos_ref, shift_ref, weight_ref, mask_ref, table_ref, own_top, own_low, phase_ref,
-    rims_out, meta_out, spec_out, pupil_out, held, rims, meta_held, send_a, recv_a, send_b, recv_b, send_s, recv_s, send_r, recv_r
+    tile_count, pos_ref, shift_ref, weight_ref, mask_hbm, table_ref, top_hbm, low_hbm, phase_ref,
+    rims_out, meta_out, spec_out, pupil_out, held, rims, meta_held, send_a, recv_a, send_b, recv_b, send_s, recv_s, send_r, recv_r,
+    rim_ref, mask_ref, own_top, own_low, load
 ):
     low, high = group_sizes(tile_count)
     tile = lax.axis_index("tile")
     src = lax.axis_index("src")
     side = src % 2
+    start = pl.multiple_of((1 - side) * (TILE_PX - HALO), HALO)
+    rim_load = pltpu.make_async_copy(mask_hbm.at[0, pl.ds(start, HALO), :], rim_ref, load.at[0])
+    rim_load.start()
+    loads = [
+        pltpu.make_async_copy(mask_hbm.at[0], mask_ref, load.at[1]),
+        pltpu.make_async_copy(top_hbm, own_top, load.at[2]),
+        pltpu.make_async_copy(low_hbm, own_low, load.at[3]),
+    ]
+    for copy in loads:
+        copy.start()
     row = lax.broadcasted_iota(jnp.int32, (8, 128), 0)
     col = lax.broadcasted_iota(jnp.int32, (8, 128), 1)
     meta = jnp.zeros((8, 128), jnp.int32)
@@ -166,10 +177,8 @@
         meta = jnp.where((row == p) & (col == 1), shift_ref[p, 1], meta)
         meta = jnp.where((row == p) & (col == 2), weight_ref[p], meta)
     meta_held[src] = meta
-    start = pl.multiple_of((1 - side) * (TILE_PX - HALO), HALO)
-    rim = jnp.dot(
-        mask_ref[0, pl.ds(start, HALO), :], table_ref[...], preferred_element_type=jnp.float32
-    )
+    rim_load.wait()
+    rim = bdot(rim_ref[...], table_ref[...])
     held[tile % low, tile // low] = rim.astype(jnp.bfloat16)
     greet(tile_count)
     high_copies = start_high(tile_count, held, send_a, recv_a)
@@ -177,10 +186,12 @@
     for copy in high_copies:
         copy.wait()
     finish_low = start_low(tile_count, held, send_b, recv_b)
+    for copy in loads:
+        copy.wait()
     spec = jnp.zeros((2 * FREQ, 2 * FREQ), jnp.float32)
     for i in range(TILE_PX // 256):
         at = slice(i * 256, (i + 1) * 256)
-        half_top, half_low = split(bdot(mask_ref[0, at, :], table_ref[...]))
+        half_top, half_low = split(bdot(mask_ref[at, :], table_ref[...]))
         spec += bdot(own_top[:, at], half_top)
         spec += bdot(own_top[:, at], half_low) + bdot(own_low[:, at], half_top)
     spec_out[...] = spec
@@ -209,12 +220,19 @@
 
 def back_kernel(
     tile_count, pos_ref, grad_ref, row_table, out_ref,
-    held, grads, total, send_a, recv_a, send_b, recv_b, send_s, recv_s
+    held, grads, total, send_a, recv_a, send_b, recv_b, send_s, recv_s, rim_table, own_table, load
 ):
     low, high = group_sizes(tile_count)
     tile = lax.axis_index("tile")
     src = lax.axis_index("src")
     src_count = lax.axis_size("src")
+    rows = out_ref.shape[0]
+    rim_at = pl.multiple_of((1 - src % 2) * (EXT_PX - HALO), HALO)
+    own_at = pl.multiple_of(HALO + src * rows, HALO)
+    rim_load = pltpu.make_async_copy(row_table.at[pl.ds(rim_at, HALO), :], rim_table, load.at[0])
+    own_load = pltpu.make_async_copy(row_table.at[pl.ds(own_at, rows), :], own_table, load.at[1])
+    rim_load.start()
+    own_load.start()
     grads[src] = grad_ref[...]
     greet(tile_count)
     for copy in start_src(grads, send_s, recv_s):
@@ -225,13 +243,12 @@
     total[:FREQ, :] = both
     total[FREQ:, :FREQ] = -both[:, FREQ:]
     total[FREQ:, FREQ:] = both[:, :FREQ]
-    rim_at = pl.multiple_of((1 - src % 2) * (EXT_PX - HALO), HALO)
-    rim_back = fdot(row_table[pl.ds(rim_at, HALO), :], total[...], HIGHEST)
+    rim_load.wait()
+    rim_back = fdot(rim_table[...], total[...], HIGHEST)
     held[tile % low, tile // low] = rim_back.astype(jnp.bfloat16)
     high_copies = start_high(tile_count, held, send_a, recv_a)
-    rows = out_ref.shape[0]
-    own_at = pl.multiple_of(HALO + src * rows, HALO)
-    out_ref[...] = fdot(row_table[pl.ds(own_at, rows), :], total[...], HIGHEST)
+    own_load.wait()
+    out_ref[...] = fdot(own_table[...], total[...], HIGHEST)
     for copy in high_copies:
         copy.wait()
     start_low(tile_count, held, send_b, recv_b)()
@@ -256,6 +273,7 @@
     metas = (lax.axis_size("src"), 8, 128)
     vmem = pl.BlockSpec(memory_space=pltpu.VMEM)
     smem = pl.BlockSpec(memory_space=pltpu.SMEM)
+    hbm = pl.BlockSpec(memory_space=pl.ANY)
     return pl.pallas_call(
         functools.partial(rim_kernel, tile_count),
         out_shape=[
@@ -264,7 +282,7 @@
             jax.ShapeDtypeStruct((2 * FREQ, 2 * FREQ), jnp.float32),
             jax.ShapeDtypeStruct((2, FREQ, FREQ), jnp.float32),
         ],
-        in_specs=[smem, smem, smem, vmem] + [vmem] * len(tables),
+        in_specs=[smem, smem, smem, hbm, vmem, hbm, hbm, vmem],
         out_specs=[vmem] * 4,
         scratch_shapes=[
             held,
@@ -273,6 +291,11 @@
             *sems,
             pltpu.SemaphoreType.DMA((1,)),
             pltpu.SemaphoreType.DMA((1,)),
+            pltpu.VMEM((HALO, TILE_PX), jnp.bfloat16),
+            pltpu.VMEM((TILE_PX, TILE_PX), jnp.bfloat16),
+            pltpu.VMEM((2 * FREQ, TILE_PX), jnp.bfloat16),
+            pltpu.VMEM((2 * FREQ, TILE_PX), jnp.bfloat16),
+            pltpu.SemaphoreType.DMA((4,)),
         ],
         compiler_params=pltpu.CompilerParams(
             collective_id=0, has_side_effects=True, vmem_limit_bytes=56 * 2**20
@@ -423,7 +446,7 @@
             jax.ShapeDtypeStruct((1, rows, TILE_PX), jnp.float32),
             jax.ShapeDtypeStruct((FREQ, wide), jnp.float32),
         ],
-        compiler_params=pltpu.CompilerParams(vmem_limit_bytes=48 * 2**20),
+        compiler_params=pltpu.CompilerParams(vmem_limit_bytes=56 * 2**20),
         cost_estimate=pl.CostEstimate(flops=10**10, bytes_accessed=10**7, transcendentals=10**6),
     )(place, metas, spec, rims, *row_tables, phase, *lines, table, table_t, target)
 
@@ -434,13 +457,18 @@
     return pl.pallas_call(
         functools.partial(back_kernel, tile_count),
         out_shape=jax.ShapeDtypeStruct((rows, 2 * FREQ), jnp.float32),
-        in_specs=[pl.BlockSpec(memory_space=pltpu.SMEM), vmem, vmem],
+        in_specs=[
+            pl.BlockSpec(memory_space=pltpu.SMEM), vmem, pl.BlockSpec(memory_space=pl.ANY)
+        ],
         out_specs=vmem,
         scratch_shapes=[
             held,
             pltpu.VMEM((lax.axis_size("src"), *grad.shape), jnp.float32),
             pltpu.VMEM((2 * FREQ, 2 * FREQ), jnp.float32),
             *sems,
+            pltpu.VMEM((HALO, 2 * FREQ), jnp.float32),
+            pltpu.VMEM((rows, 2 * FREQ), jnp.float32),
+            pltpu.SemaphoreType.DMA((2,)),
         ],
         compiler_params=pltpu.CompilerParams(
             collective_id=1, has_side_effects=True, vmem_limit_bytes=56 * 2**20

time: 64.6 us -> 58.1 us (0.90)
  local copies, waits for them, and re-layouts: 7.17 us -> 0.01 us
  Pallas kernels: 53.3 us -> 54.3 us
    unnamed x26 -> x2, local copies, waits for them, and re-layouts: 7.17 us -> 0.01 us
    pallas_call x1, Pallas kernels: 15.3 us -> 16.7 us  [image_step(): pl.pallas_call(functools.partial(image_kernel, sources_total, scale_facto...]
where the time goes in v3:
time: 58.1 us; the launch traced here: 57.8 us
  Pallas kernels  54.3 us (93%)
  matrix products  2.8 us (5%)
  between operations  0.67 us (1%)
    pallas_call x1, Pallas kernels, exchange_rims(): pl.pallas_call(functools.partial(rim_kernel, tile_count), out_shape=[jax....  19.9 us
    pallas_call x1, Pallas kernels, exchange_back(): pl.pallas_call(functools.partial(back_kernel, tile_count), out_shape=jax....  17.6 us
    pallas_call x1, Pallas kernels, image_step(): pl.pallas_call(functools.partial(image_kernel, sources_total, scale_facto...  16.7 us
    dot_general x1, matrix products, per_device(): jnp.dot(back_rows.astype(jnp.bfloat16), last_table, preferred_element_typ...  2.8 us

profile of v3, /device:TPU:1, one launch (start us, length us, event | category | flops | bytes accessed | tf_op | source)
XLA Modules:
  0.0 57.8 jit_solution(121950709375891980)
XLA Ops:
  0.6 19.9 %shard_map.176 = (bf16[2,64,256]{2,1,0:T(8,128)(2,1)}, s32[2,8,128]{2,1,0:T(8,128)}, f32[256,256]{1,0:T(8,128)}, f32[2,128,128]{2,1,0:T(8,128)}) custom-call(s32[16]{0:T(128)} %pos_ref.3, s32[2,2]{1,0:T(2,128)} %shift_ref.1, s32[2]{0:T(128)} %weight_ref.1, bf16[1,1024,1024]{2,1,0:T(8,128)(2,1)} %mask_hbm.1, bf16[1024,256]{1,0:T(8,128)(2,1)} %constant.28.clone.table_ref, ...), custom_call_target="tpu_custom_call" | custom-call | flops 600000000 | bytes 4194304 | tf_op jit(solution)/shard_map/pallas_call | solution.py:277
  20.6 16.7 %shard_map.177 = (f32[1,512,1024]{2,1,0:T(8,128)}, f32[128,256]{1,0:T(8,128)}) custom-call(s32[1]{0:T(128)} %bitcast.place_ref, s32[2,8,128]{2,1,0:T(8,128)} %get-tuple-element.8.meta_ref, f32[256,256]{1,0:T(8,128)} %get-tuple-element.9.spec_ref, bf16[2,64,256]{2,1,0:T(8,128)(2,1)} %get-tuple-element.10.rims_ref, bf16[256,128]{1,0:T(8,128)(2,1)} %constant.31.clone.rim_top, ...), custom_call_target="tpu_custom_call" | custom-call | flops 10000000000 | bytes 10000000 | tf_op jit(solution)/shard_map/pallas_call | solution.py:442
  37.3 0.0 copy-start
  37.3 17.6 %shard_map.178 = f32[512,256]{1,0:T(8,128)} custom-call(s32[16]{0:T(128)} %pos_ref.3, f32[128,256]{1,0:T(8,128)} %get-tuple-element.13.grad_ref, f32[1152,256]{1,0:T(8,128)} %constant.36.clone.row_table), custom_call_target="tpu_custom_call" | custom-call | flops 100000000 | bytes 2097152 | tf_op jit(solution)/shard_map/pallas_call | solution.py:457
  54.9 0.0 copy-done
  54.9 2.8 %multiply_bitcast_fusion = f32[1,512,1024]{2,1,0:T(8,128)} fusion(bf16[256,1024]{1,0:T(8,128)(2,1)S(1)} %copy-done, f32[512,256]{1,0:T(8,128)} %shard_map.178), kind=kOutput, calls=%fused_computation | convolution fusion | flops 269090816 | bytes 3145728 | tf_op jit(solution)/shard_map/dot_general | solution.py:511
Async XLA Ops:
  37.3 17.7 %copy-start = (bf16[256,1024]{1,0:T(8,128)(2,1)S(1)}, bf16[256,1024]{1,0:T(8,128)(2,1)}, u32[]{:S(2)}) copy-start(bf16[256,1024]{1,0:T(8,128)(2,1)} %constant.37.clone) | copy-start | bytes 1572868
